TPU v7x, 256 devices: a whole 4x4x8 slice. The times are simulated.
256 devices in a mesh: section: 16 (over z, core), tp: 16 (over x, y).
Axes of the slice: x: 4, y: 4, z: 8, core: 2. Of those that a mesh axis runs over, the one named last changes fastest.
Arguments:
- patches: bfloat16 [1024, 1664], P(('section', 'tp')), may hold values from -6 to 6
- vit_gain: float32 [1664], replicated, may hold values from 0.1 to 1.9
- vit_up: bfloat16 [1664, 4096], P(None, 'tp'), may hold values from -0.15625 to 0.15625
- vit_down: bfloat16 [4096, 1664], P('tp'), may hold values from -0.1875 to 0.1875
- project: bfloat16 [1664, 8192], P(None, 'tp'), may hold values from -0.4375 to 0.4375
- text: bfloat16 [256, 8192], P(None, 'tp'), may hold values from -6 to 6
- image_counts: int32 [16], replicated, may hold values from 1 to 16, as said below
- image_dest: int32 [16, 16], replicated, may hold values from 0 to 255, as said below
- layer_gain: bfloat16 [16, 8192], P('section', 'tp'), may hold values from 0.25 to 1.75
- layer_weight: bfloat16 [16, 8192, 8192], P('section', None, 'tp'), may hold values from -0.0625 to 0.0625
Outputs:
- section_outputs: bfloat16 [16, 8, 32, 8192], P('section', None, None, 'tp')
Inputs may be any that keep to these rules, and one draw needn't show every extreme that they name: Section s uses the first image_counts[s] of its 16 slots; at least one section uses all 16. `image_dest`: all entries are distinct.
All inputs are finite; a program needn't handle non-finite values.
Results may differ from a plain program's by a relative error of at most 0.024.
Values may be sent and summed in bfloat16 or wider, within the bound.
A program may use at most 64 MiB of HBM per device.

v0:
```python
import jax
import jax.numpy as jnp
from jax import lax
from jax.sharding import PartitionSpec as P

D = 8192
POOL = 4
MB = 8


EPSILON = 1e-05


def passed_along(value, axis, steps):
    count = lax.axis_size(axis)
    leading, last = (max(0, -steps), min(count, count - steps))
    return lax.ppermute(value, axis, [(source, source + steps) for source in range(leading, last)])


def encoder_terms(patch_block, vit_gain, vit_up, vit_down):
    values = patch_block.astype(jnp.float32)
    centre = jnp.mean(values, axis=1, keepdims=True)
    centred = values - centre
    spread = jnp.mean(centred * centred, axis=1, keepdims=True)
    normed = (centred * lax.rsqrt(spread + EPSILON) * vit_gain).astype(jnp.bfloat16)
    hidden = jax.nn.gelu(
        jnp.dot(normed, vit_up, preferred_element_type=jnp.float32), approximate=True
    ).astype(jnp.bfloat16)
    return jnp.dot(hidden, vit_down, preferred_element_type=jnp.float32)


def merge_rows(encoded):
    return jnp.mean(encoded.reshape(-1, POOL, encoded.shape[1]), axis=1).astype(jnp.bfloat16)


def shards(
    patches,
    vit_gain,
    vit_up,
    vit_down,
    project,
    text,
    image_counts,
    image_dest,
    layer_gain,
    layer_weight,
):
    section = lax.axis_index("section")
    section_count = lax.axis_size("section")
    whole = lax.all_gather(patches, "tp", axis=0, tiled=True)
    total = lax.psum(encoder_terms(whole, vit_gain, vit_up, vit_down), "tp")
    pooled = merge_rows(whole.astype(jnp.float32) + total)
    embeds = jnp.dot(pooled, project, preferred_element_type=jnp.float32).astype(jnp.bfloat16)
    slot_count = embeds.shape[0]
    row_count = text.shape[0]
    positions = jnp.arange(row_count, dtype=jnp.int32)
    slots = jnp.arange(slot_count, dtype=jnp.int32)
    contract = (((0,), (0,)), ((), ()))
    own_dest = lax.dynamic_index_in_dim(image_dest, section, 0, keepdims=False)
    own_count = lax.dynamic_index_in_dim(image_counts, section, 0, keepdims=False)
    onehot = ((own_dest[:, None] == positions[None, :]) & (slots < own_count)[:, None]).astype(
        jnp.float32
    )
    local_placed = lax.dot_general(
        onehot, embeds.astype(jnp.float32), contract, precision=lax.Precision.HIGHEST
    )
    placed = lax.psum(local_placed, "section")
    width_local = text.shape[1]
    start_rows = (
        (text.astype(jnp.float32) + placed).astype(jnp.bfloat16).reshape(MB, -1, width_local)
    )
    seq_len = start_rows.shape[1]
    weight = layer_weight[0]

    def tick_step(carry, tick):
        incoming, outputs = carry
        first = lax.dynamic_index_in_dim(start_rows, jnp.clip(tick, 0, MB - 1), 0, keepdims=False)
        active = jnp.where(section == 0, first, incoming)
        part = lax.all_gather(active, "tp", axis=1, tiled=True)
        part_gain = lax.all_gather(layer_gain, "tp", axis=1, tiled=True)
        part_f = part.astype(jnp.float32)
        scaled = (part_f * part_gain.astype(jnp.float32)).astype(jnp.bfloat16)
        product = jnp.dot(scaled, weight, preferred_element_type=jnp.float32)
        squares = jnp.sum(part_f * part_f, axis=1, keepdims=True)
        product, squares = (product, squares)
        scale = lax.rsqrt(squares / D + EPSILON)
        result = (active.astype(jnp.float32) + product * scale).astype(jnp.bfloat16)
        micro = tick - section
        valid = (micro >= 0) & (micro < MB)
        written = lax.dynamic_update_index_in_dim(outputs, result, jnp.clip(micro, 0, MB - 1), 0)
        outputs = jnp.where(valid, written, outputs)
        incoming = passed_along(result, "section", 1)
        return ((incoming, outputs), None)

    ticks = MB + section_count - 1
    start_carry = (
        jnp.zeros((seq_len, width_local), jnp.bfloat16),
        jnp.zeros((MB, seq_len, width_local), jnp.bfloat16),
    )
    (final_incoming, outputs), _ = lax.scan(
        tick_step, start_carry, jnp.arange(ticks, dtype=jnp.int32)
    )
    return outputs[None]


def solution(mesh):
    in_specs = (
        P(("section", "tp"), None),
        P(),
        P(None, "tp"),
        P("tp", None),
        P(None, "tp"),
        P(None, "tp"),
        P(),
        P(),
        P("section", "tp"),
        P("section", None, "tp"),
    )
    out_specs = P("section", None, None, "tp")
    return jax.shard_map(shards, mesh=mesh, in_specs=in_specs, out_specs=out_specs, check_vma=False)
```

profile of v0, /device:TPU:128, one launch (start us, length us, event | category | flops | bytes accessed | tf_op | source)
XLA Modules:
  0.0 1585.7 jit_solution(17519278626261541767)
XLA Ops:
  6.5 24.2 %all-gather = bf16[16,4,1664]{2,1,0:T(4,128)(2,1)S(1)} all-gather(bf16[1,4,1664]{2,1,0:T(4,128)(2,1)} %bitcast.33), channel_id=1, replica_groups=mesh['section'=16,'tp'=16] {'tp'}, dimensions={0}, use_global_device_ids=true | all-gather | bytes 226304 | tf_op jit(solution)/shard_map/all_gather | solution.py:50
  36.9 91.4 %all-reduce.3.cloned.1.call-done = f32[64,1664]{1,0:T(8,128)} async-done(((f32[64,1664]{1,0:T(8,128)}), f32[64,1664]{1,0:T(8,128)}) %all-reduce.3.cloned.1.call-update) | async-done | bytes 426000 | tf_op jit(solution)/shard_map/psum | solution.py:51
  131.2 107.5 %all-reduce.5.cloned.1.call-done = f32[256,512]{1,0:T(8,128)} async-done(((f32[256,512]{1,0:T(8,128)}), f32[256,512]{1,0:T(8,128)}) %all-reduce.5.cloned.1.call-update) | async-done | bytes 524304 | tf_op jit(solution)/shard_map/psum | solution.py:67
  239.9 1338.2 %while.13 = (s32[]{:T(128)}, bf16[32,512]{1,0:T(8,128)(2,1)S(1)}, bf16[8,32,512]{2,1,0:T(8,128)(2,1)S(1)}, pred[]{:T(512)}, s32[23]{0:T(128)S(1)}, /*index=5*/bf...) while((s32[]{:T(128)}, bf16[32,512]{1,0:T(8,128)(2,1)S(1)}, ...), condition=%wide.region_7.8_spmd, body=%wide.region_5.7_spmd.sunk | while | flops 270114848 | bytes 10455180 | solution.py:100
  242.0 24.0 %all_gather.14 = bf16[32,8192]{1,0:T(8,128)(2,1)S(1)} all-gather(bf16[32,512]{1,0:T(8,128)(2,1)S(1)} %bitcast_select_fusion.3), channel_id=1, replica_groups=mesh['section'=16,'tp'=16] {'tp'}, dimensions={1}, use_global_device_ids=true | all-gather | bytes 557056 | tf_op jit(solution)/shard_map/while/body/eval_jaxpr/all_gather | solution.py:79
  266.3 22.6 %all_gather.15 = bf16[1,8192]{1,0:T(2,128)(2,1)S(1)} all-gather(bf16[1,512]{1,0:T(2,128)(2,1)S(1)} %get-tuple-element.196), channel_id=1, replica_groups=mesh['section'=16,'tp'=16] {'tp'}, dimensions={1}, use_global_device_ids=true | all-gather | bytes 17408 | tf_op jit(solution)/shard_map/while/body/eval_jaxpr/all_gather | solution.py:80
  302.3 21.8 %all_gather.14 = bf16[32,8192]{1,0:T(8,128)(2,1)S(1)} all-gather(bf16[32,512]{1,0:T(8,128)(2,1)S(1)} %bitcast_select_fusion.3), channel_id=1, replica_groups=mesh['section'=16,'tp'=16] {'tp'}, dimensions={1}, use_global_device_ids=true | all-gather | bytes 557056 | tf_op jit(solution)/shard_map/while/body/eval_jaxpr/all_gather | solution.py:79
  324.4 22.5 %all_gather.15 = bf16[1,8192]{1,0:T(2,128)(2,1)S(1)} all-gather(bf16[1,512]{1,0:T(2,128)(2,1)S(1)} %get-tuple-element.196), channel_id=1, replica_groups=mesh['section'=16,'tp'=16] {'tp'}, dimensions={1}, use_global_device_ids=true | all-gather | bytes 17408 | tf_op jit(solution)/shard_map/while/body/eval_jaxpr/all_gather | solution.py:80
  347.0 4.9 fusion.45
  360.4 21.8 %all_gather.14 = bf16[32,8192]{1,0:T(8,128)(2,1)S(1)} all-gather(bf16[32,512]{1,0:T(8,128)(2,1)S(1)} %bitcast_select_fusion.3), channel_id=1, replica_groups=mesh['section'=16,'tp'=16] {'tp'}, dimensions={1}, use_global_device_ids=true | all-gather | bytes 557056 | tf_op jit(solution)/shard_map/while/body/eval_jaxpr/all_gather | solution.py:79
  382.5 22.5 %all_gather.15 = bf16[1,8192]{1,0:T(2,128)(2,1)S(1)} all-gather(bf16[1,512]{1,0:T(2,128)(2,1)S(1)} %get-tuple-element.196), channel_id=1, replica_groups=mesh['section'=16,'tp'=16] {'tp'}, dimensions={1}, use_global_device_ids=true | all-gather | bytes 17408 | tf_op jit(solution)/shard_map/while/body/eval_jaxpr/all_gather | solution.py:80
  405.1 4.9 fusion.45
  418.5 21.8 %all_gather.14 = bf16[32,8192]{1,0:T(8,128)(2,1)S(1)} all-gather(bf16[32,512]{1,0:T(8,128)(2,1)S(1)} %bitcast_select_fusion.3), channel_id=1, replica_groups=mesh['section'=16,'tp'=16] {'tp'}, dimensions={1}, use_global_device_ids=true | all-gather | bytes 557056 | tf_op jit(solution)/shard_map/while/body/eval_jaxpr/all_gather | solution.py:79
  440.5 22.5 %all_gather.15 = bf16[1,8192]{1,0:T(2,128)(2,1)S(1)} all-gather(bf16[1,512]{1,0:T(2,128)(2,1)S(1)} %get-tuple-element.196), channel_id=1, replica_groups=mesh['section'=16,'tp'=16] {'tp'}, dimensions={1}, use_global_device_ids=true | all-gather | bytes 17408 | tf_op jit(solution)/shard_map/while/body/eval_jaxpr/all_gather | solution.py:80
  463.1 4.9 fusion.45
  476.6 21.8 %all_gather.14 = bf16[32,8192]{1,0:T(8,128)(2,1)S(1)} all-gather(bf16[32,512]{1,0:T(8,128)(2,1)S(1)} %bitcast_select_fusion.3), channel_id=1, replica_groups=mesh['section'=16,'tp'=16] {'tp'}, dimensions={1}, use_global_device_ids=true | all-gather | bytes 557056 | tf_op jit(solution)/shard_map/while/body/eval_jaxpr/all_gather | solution.py:79
  498.6 22.5 %all_gather.15 = bf16[1,8192]{1,0:T(2,128)(2,1)S(1)} all-gather(bf16[1,512]{1,0:T(2,128)(2,1)S(1)} %get-tuple-element.196), channel_id=1, replica_groups=mesh['section'=16,'tp'=16] {'tp'}, dimensions={1}, use_global_device_ids=true | all-gather | bytes 17408 | tf_op jit(solution)/shard_map/while/body/eval_jaxpr/all_gather | solution.py:80
  521.2 4.9 fusion.45
  534.6 21.8 %all_gather.14 = bf16[32,8192]{1,0:T(8,128)(2,1)S(1)} all-gather(bf16[32,512]{1,0:T(8,128)(2,1)S(1)} %bitcast_select_fusion.3), channel_id=1, replica_groups=mesh['section'=16,'tp'=16] {'tp'}, dimensions={1}, use_global_device_ids=true | all-gather | bytes 557056 | tf_op jit(solution)/shard_map/while/body/eval_jaxpr/all_gather | solution.py:79
  556.7 22.5 %all_gather.15 = bf16[1,8192]{1,0:T(2,128)(2,1)S(1)} all-gather(bf16[1,512]{1,0:T(2,128)(2,1)S(1)} %get-tuple-element.196), channel_id=1, replica_groups=mesh['section'=16,'tp'=16] {'tp'}, dimensions={1}, use_global_device_ids=true | all-gather | bytes 17408 | tf_op jit(solution)/shard_map/while/body/eval_jaxpr/all_gather | solution.py:80
  579.3 4.9 fusion.45
  592.7 21.8 %all_gather.14 = bf16[32,8192]{1,0:T(8,128)(2,1)S(1)} all-gather(bf16[32,512]{1,0:T(8,128)(2,1)S(1)} %bitcast_select_fusion.3), channel_id=1, replica_groups=mesh['section'=16,'tp'=16] {'tp'}, dimensions={1}, use_global_device_ids=true | all-gather | bytes 557056 | tf_op jit(solution)/shard_map/while/body/eval_jaxpr/all_gather | solution.py:79
  614.8 22.5 %all_gather.15 = bf16[1,8192]{1,0:T(2,128)(2,1)S(1)} all-gather(bf16[1,512]{1,0:T(2,128)(2,1)S(1)} %get-tuple-element.196), channel_id=1, replica_groups=mesh['section'=16,'tp'=16] {'tp'}, dimensions={1}, use_global_device_ids=true | all-gather | bytes 17408 | tf_op jit(solution)/shard_map/while/body/eval_jaxpr/all_gather | solution.py:80
  637.4 4.9 fusion.45
  650.8 21.8 %all_gather.14 = bf16[32,8192]{1,0:T(8,128)(2,1)S(1)} all-gather(bf16[32,512]{1,0:T(8,128)(2,1)S(1)} %bitcast_select_fusion.3), channel_id=1, replica_groups=mesh['section'=16,'tp'=16] {'tp'}, dimensions={1}, use_global_device_ids=true | all-gather | bytes 557056 | tf_op jit(solution)/shard_map/while/body/eval_jaxpr/all_gather | solution.py:79
  672.9 22.5 %all_gather.15 = bf16[1,8192]{1,0:T(2,128)(2,1)S(1)} all-gather(bf16[1,512]{1,0:T(2,128)(2,1)S(1)} %get-tuple-element.196), channel_id=1, replica_groups=mesh['section'=16,'tp'=16] {'tp'}, dimensions={1}, use_global_device_ids=true | all-gather | bytes 17408 | tf_op jit(solution)/shard_map/while/body/eval_jaxpr/all_gather | solution.py:80
  695.5 4.9 fusion.45
  708.9 21.8 %all_gather.14 = bf16[32,8192]{1,0:T(8,128)(2,1)S(1)} all-gather(bf16[32,512]{1,0:T(8,128)(2,1)S(1)} %bitcast_select_fusion.3), channel_id=1, replica_groups=mesh['section'=16,'tp'=16] {'tp'}, dimensions={1}, use_global_device_ids=true | all-gather | bytes 557056 | tf_op jit(solution)/shard_map/while/body/eval_jaxpr/all_gather | solution.py:79
  731.0 22.5 %all_gather.15 = bf16[1,8192]{1,0:T(2,128)(2,1)S(1)} all-gather(bf16[1,512]{1,0:T(2,128)(2,1)S(1)} %get-tuple-element.196), channel_id=1, replica_groups=mesh['section'=16,'tp'=16] {'tp'}, dimensions={1}, use_global_device_ids=true | all-gather | bytes 17408 | tf_op jit(solution)/shard_map/while/body/eval_jaxpr/all_gather | solution.py:80
  753.6 4.9 fusion.45
  767.0 21.8 %all_gather.14 = bf16[32,8192]{1,0:T(8,128)(2,1)S(1)} all-gather(bf16[32,512]{1,0:T(8,128)(2,1)S(1)} %bitcast_select_fusion.3), channel_id=1, replica_groups=mesh['section'=16,'tp'=16] {'tp'}, dimensions={1}, use_global_device_ids=true | all-gather | bytes 557056 | tf_op jit(solution)/shard_map/while/body/eval_jaxpr/all_gather | solution.py:79
  789.1 22.5 %all_gather.15 = bf16[1,8192]{1,0:T(2,128)(2,1)S(1)} all-gather(bf16[1,512]{1,0:T(2,128)(2,1)S(1)} %get-tuple-element.196), channel_id=1, replica_groups=mesh['section'=16,'tp'=16] {'tp'}, dimensions={1}, use_global_device_ids=true | all-gather | bytes 17408 | tf_op jit(solution)/shard_map/while/body/eval_jaxpr/all_gather | solution.py:80
  811.7 4.9 fusion.45
  825.1 21.8 %all_gather.14 = bf16[32,8192]{1,0:T(8,128)(2,1)S(1)} all-gather(bf16[32,512]{1,0:T(8,128)(2,1)S(1)} %bitcast_select_fusion.3), channel_id=1, replica_groups=mesh['section'=16,'tp'=16] {'tp'}, dimensions={1}, use_global_device_ids=true | all-gather | bytes 557056 | tf_op jit(solution)/shard_map/while/body/eval_jaxpr/all_gather | solution.py:79
  847.2 22.5 %all_gather.15 = bf16[1,8192]{1,0:T(2,128)(2,1)S(1)} all-gather(bf16[1,512]{1,0:T(2,128)(2,1)S(1)} %get-tuple-element.196), channel_id=1, replica_groups=mesh['section'=16,'tp'=16] {'tp'}, dimensions={1}, use_global_device_ids=true | all-gather | bytes 17408 | tf_op jit(solution)/shard_map/while/body/eval_jaxpr/all_gather | solution.py:80
  869.8 4.9 fusion.45
  883.2 21.8 %all_gather.14 = bf16[32,8192]{1,0:T(8,128)(2,1)S(1)} all-gather(bf16[32,512]{1,0:T(8,128)(2,1)S(1)} %bitcast_select_fusion.3), channel_id=1, replica_groups=mesh['section'=16,'tp'=16] {'tp'}, dimensions={1}, use_global_device_ids=true | all-gather | bytes 557056 | tf_op jit(solution)/shard_map/while/body/eval_jaxpr/all_gather | solution.py:79
  905.3 22.5 %all_gather.15 = bf16[1,8192]{1,0:T(2,128)(2,1)S(1)} all-gather(bf16[1,512]{1,0:T(2,128)(2,1)S(1)} %get-tuple-element.196), channel_id=1, replica_groups=mesh['section'=16,'tp'=16] {'tp'}, dimensions={1}, use_global_device_ids=true | all-gather | bytes 17408 | tf_op jit(solution)/shard_map/while/body/eval_jaxpr/all_gather | solution.py:80
  927.8 4.9 fusion.45
  941.3 21.8 %all_gather.14 = bf16[32,8192]{1,0:T(8,128)(2,1)S(1)} all-gather(bf16[32,512]{1,0:T(8,128)(2,1)S(1)} %bitcast_select_fusion.3), channel_id=1, replica_groups=mesh['section'=16,'tp'=16] {'tp'}, dimensions={1}, use_global_device_ids=true | all-gather | bytes 557056 | tf_op jit(solution)/shard_map/while/body/eval_jaxpr/all_gather | solution.py:79
  963.3 22.5 %all_gather.15 = bf16[1,8192]{1,0:T(2,128)(2,1)S(1)} all-gather(bf16[1,512]{1,0:T(2,128)(2,1)S(1)} %get-tuple-element.196), channel_id=1, replica_groups=mesh['section'=16,'tp'=16] {'tp'}, dimensions={1}, use_global_device_ids=true | all-gather | bytes 17408 | tf_op jit(solution)/shard_map/while/body/eval_jaxpr/all_gather | solution.py:80
  985.9 4.9 fusion.45
  999.4 21.8 %all_gather.14 = bf16[32,8192]{1,0:T(8,128)(2,1)S(1)} all-gather(bf16[32,512]{1,0:T(8,128)(2,1)S(1)} %bitcast_select_fusion.3), channel_id=1, replica_groups=mesh['section'=16,'tp'=16] {'tp'}, dimensions={1}, use_global_device_ids=true | all-gather | bytes 557056 | tf_op jit(solution)/shard_map/while/body/eval_jaxpr/all_gather | solution.py:79
  1021.4 22.5 %all_gather.15 = bf16[1,8192]{1,0:T(2,128)(2,1)S(1)} all-gather(bf16[1,512]{1,0:T(2,128)(2,1)S(1)} %get-tuple-element.196), channel_id=1, replica_groups=mesh['section'=16,'tp'=16] {'tp'}, dimensions={1}, use_global_device_ids=true | all-gather | bytes 17408 | tf_op jit(solution)/shard_map/while/body/eval_jaxpr/all_gather | solution.py:80
  1044.0 4.9 fusion.45
  1057.4 21.8 %all_gather.14 = bf16[32,8192]{1,0:T(8,128)(2,1)S(1)} all-gather(bf16[32,512]{1,0:T(8,128)(2,1)S(1)} %bitcast_select_fusion.3), channel_id=1, replica_groups=mesh['section'=16,'tp'=16] {'tp'}, dimensions={1}, use_global_device_ids=true | all-gather | bytes 557056 | tf_op jit(solution)/shard_map/while/body/eval_jaxpr/all_gather | solution.py:79
  1079.5 22.5 %all_gather.15 = bf16[1,8192]{1,0:T(2,128)(2,1)S(1)} all-gather(bf16[1,512]{1,0:T(2,128)(2,1)S(1)} %get-tuple-element.196), channel_id=1, replica_groups=mesh['section'=16,'tp'=16] {'tp'}, dimensions={1}, use_global_device_ids=true | all-gather | bytes 17408 | tf_op jit(solution)/shard_map/while/body/eval_jaxpr/all_gather | solution.py:80
  1115.5 21.8 %all_gather.14 = bf16[32,8192]{1,0:T(8,128)(2,1)S(1)} all-gather(bf16[32,512]{1,0:T(8,128)(2,1)S(1)} %bitcast_select_fusion.3), channel_id=1, replica_groups=mesh['section'=16,'tp'=16] {'tp'}, dimensions={1}, use_global_device_ids=true | all-gather | bytes 557056 | tf_op jit(solution)/shard_map/while/body/eval_jaxpr/all_gather | solution.py:79
  1137.6 22.5 %all_gather.15 = bf16[1,8192]{1,0:T(2,128)(2,1)S(1)} all-gather(bf16[1,512]{1,0:T(2,128)(2,1)S(1)} %get-tuple-element.196), channel_id=1, replica_groups=mesh['section'=16,'tp'=16] {'tp'}, dimensions={1}, use_global_device_ids=true | all-gather | bytes 17408 | tf_op jit(solution)/shard_map/while/body/eval_jaxpr/all_gather | solution.py:80
  1173.6 21.8 %all_gather.14 = bf16[32,8192]{1,0:T(8,128)(2,1)S(1)} all-gather(bf16[32,512]{1,0:T(8,128)(2,1)S(1)} %bitcast_select_fusion.3), channel_id=1, replica_groups=mesh['section'=16,'tp'=16] {'tp'}, dimensions={1}, use_global_device_ids=true | all-gather | bytes 557056 | tf_op jit(solution)/shard_map/while/body/eval_jaxpr/all_gather | solution.py:79
  1195.7 22.5 %all_gather.15 = bf16[1,8192]{1,0:T(2,128)(2,1)S(1)} all-gather(bf16[1,512]{1,0:T(2,128)(2,1)S(1)} %get-tuple-element.196), channel_id=1, replica_groups=mesh['section'=16,'tp'=16] {'tp'}, dimensions={1}, use_global_device_ids=true | all-gather | bytes 17408 | tf_op jit(solution)/shard_map/while/body/eval_jaxpr/all_gather | solution.py:80
  1231.7 21.8 %all_gather.14 = bf16[32,8192]{1,0:T(8,128)(2,1)S(1)} all-gather(bf16[32,512]{1,0:T(8,128)(2,1)S(1)} %bitcast_select_fusion.3), channel_id=1, replica_groups=mesh['section'=16,'tp'=16] {'tp'}, dimensions={1}, use_global_device_ids=true | all-gather | bytes 557056 | tf_op jit(solution)/shard_map/while/body/eval_jaxpr/all_gather | solution.py:79
  1253.8 22.5 %all_gather.15 = bf16[1,8192]{1,0:T(2,128)(2,1)S(1)} all-gather(bf16[1,512]{1,0:T(2,128)(2,1)S(1)} %get-tuple-element.196), channel_id=1, replica_groups=mesh['section'=16,'tp'=16] {'tp'}, dimensions={1}, use_global_device_ids=true | all-gather | bytes 17408 | tf_op jit(solution)/shard_map/while/body/eval_jaxpr/all_gather | solution.py:80
  1276.4 4.9 fusion.45
  1289.8 21.8 %all_gather.14 = bf16[32,8192]{1,0:T(8,128)(2,1)S(1)} all-gather(bf16[32,512]{1,0:T(8,128)(2,1)S(1)} %bitcast_select_fusion.3), channel_id=1, replica_groups=mesh['section'=16,'tp'=16] {'tp'}, dimensions={1}, use_global_device_ids=true | all-gather | bytes 557056 | tf_op jit(solution)/shard_map/while/body/eval_jaxpr/all_gather | solution.py:79
  1311.9 22.5 %all_gather.15 = bf16[1,8192]{1,0:T(2,128)(2,1)S(1)} all-gather(bf16[1,512]{1,0:T(2,128)(2,1)S(1)} %get-tuple-element.196), channel_id=1, replica_groups=mesh['section'=16,'tp'=16] {'tp'}, dimensions={1}, use_global_device_ids=true | all-gather | bytes 17408 | tf_op jit(solution)/shard_map/while/body/eval_jaxpr/all_gather | solution.py:80
  1347.9 21.8 %all_gather.14 = bf16[32,8192]{1,0:T(8,128)(2,1)S(1)} all-gather(bf16[32,512]{1,0:T(8,128)(2,1)S(1)} %bitcast_select_fusion.3), channel_id=1, replica_groups=mesh['section'=16,'tp'=16] {'tp'}, dimensions={1}, use_global_device_ids=true | all-gather | bytes 557056 | tf_op jit(solution)/shard_map/while/body/eval_jaxpr/all_gather | solution.py:79
  1370.0 22.5 %all_gather.15 = bf16[1,8192]{1,0:T(2,128)(2,1)S(1)} all-gather(bf16[1,512]{1,0:T(2,128)(2,1)S(1)} %get-tuple-element.196), channel_id=1, replica_groups=mesh['section'=16,'tp'=16] {'tp'}, dimensions={1}, use_global_device_ids=true | all-gather | bytes 17408 | tf_op jit(solution)/shard_map/while/body/eval_jaxpr/all_gather | solution.py:80
  1406.0 21.8 %all_gather.14 = bf16[32,8192]{1,0:T(8,128)(2,1)S(1)} all-gather(bf16[32,512]{1,0:T(8,128)(2,1)S(1)} %bitcast_select_fusion.3), channel_id=1, replica_groups=mesh['section'=16,'tp'=16] {'tp'}, dimensions={1}, use_global_device_ids=true | all-gather | bytes 557056 | tf_op jit(solution)/shard_map/while/body/eval_jaxpr/all_gather | solution.py:79
  1428.0 22.5 %all_gather.15 = bf16[1,8192]{1,0:T(2,128)(2,1)S(1)} all-gather(bf16[1,512]{1,0:T(2,128)(2,1)S(1)} %get-tuple-element.196), channel_id=1, replica_groups=mesh['section'=16,'tp'=16] {'tp'}, dimensions={1}, use_global_device_ids=true | all-gather | bytes 17408 | tf_op jit(solution)/shard_map/while/body/eval_jaxpr/all_gather | solution.py:80
  1464.1 21.8 %all_gather.14 = bf16[32,8192]{1,0:T(8,128)(2,1)S(1)} all-gather(bf16[32,512]{1,0:T(8,128)(2,1)S(1)} %bitcast_select_fusion.3), channel_id=1, replica_groups=mesh['section'=16,'tp'=16] {'tp'}, dimensions={1}, use_global_device_ids=true | all-gather | bytes 557056 | tf_op jit(solution)/shard_map/while/body/eval_jaxpr/all_gather | solution.py:79
  1486.1 22.5 %all_gather.15 = bf16[1,8192]{1,0:T(2,128)(2,1)S(1)} all-gather(bf16[1,512]{1,0:T(2,128)(2,1)S(1)} %get-tuple-element.196), channel_id=1, replica_groups=mesh['section'=16,'tp'=16] {'tp'}, dimensions={1}, use_global_device_ids=true | all-gather | bytes 17408 | tf_op jit(solution)/shard_map/while/body/eval_jaxpr/all_gather | solution.py:80
  1522.1 21.8 %all_gather.14 = bf16[32,8192]{1,0:T(8,128)(2,1)S(1)} all-gather(bf16[32,512]{1,0:T(8,128)(2,1)S(1)} %bitcast_select_fusion.3), channel_id=1, replica_groups=mesh['section'=16,'tp'=16] {'tp'}, dimensions={1}, use_global_device_ids=true | all-gather | bytes 557056 | tf_op jit(solution)/shard_map/while/body/eval_jaxpr/all_gather | solution.py:79
  1544.2 22.5 %all_gather.15 = bf16[1,8192]{1,0:T(2,128)(2,1)S(1)} all-gather(bf16[1,512]{1,0:T(2,128)(2,1)S(1)} %get-tuple-element.196), channel_id=1, replica_groups=mesh['section'=16,'tp'=16] {'tp'}, dimensions={1}, use_global_device_ids=true | all-gather | bytes 17408 | tf_op jit(solution)/shard_map/while/body/eval_jaxpr/all_gather | solution.py:80
  (201 shorter events, 224.7 us)
Async XLA Ops:
  6.5 123.2 %copy-start = (bf16[1664,512]{1,0:T(8,128)(2,1)S(1)}, bf16[1664,512]{1,0:T(8,128)(2,1)}, u32[]{:S(2)}) copy-start(bf16[1664,512]{1,0:T(8,128)(2,1)} %param.16) | copy-start | bytes 5111812
  6.5 232.2 %copy-start.2 = (bf16[256,512]{1,0:T(8,128)(2,1)S(1)}, bf16[256,512]{1,0:T(8,128)(2,1)}, u32[]{:S(2)}) copy-start(bf16[256,512]{1,0:T(8,128)(2,1)} %param.17) | copy-start | bytes 786436
  6.5 233.4 %copy-start.3 = (bf16[1,512]{1,0:T(2,128)(2,1)S(1)}, bf16[1,512]{1,0:T(2,128)(2,1)}, u32[]{:S(2)}) copy-start(bf16[1,512]{1,0:T(2,128)(2,1)} %param.20) | copy-start | bytes 3076
  6.5 121.7 %all-reduce.3.cloned.1.call-start = ((), (), s32[]{:S(2)}) async-start(), calls=%async_computation | async-start | bytes 851968 | tf_op jit(solution)/shard_map/psum | solution.py:51
  34.2 204.5 %all-reduce.5.cloned.1.call-start = ((), (), s32[]{:S(2)}) async-start(), calls=%async_computation.1 | async-start | bytes 1048576 | tf_op jit(solution)/shard_map/psum | solution.py:67
  293.8 6.4 collective-permute-start
  351.9 6.4 collective-permute-start
  409.9 6.4 collective-permute-start
  468.0 6.4 collective-permute-start
  526.1 6.4 collective-permute-start
  584.2 6.4 collective-permute-start
  642.3 6.4 collective-permute-start
  700.4 6.4 collective-permute-start
  758.5 6.4 collective-permute-start
  816.6 6.4 collective-permute-start
  874.7 6.4 collective-permute-start
  932.7 6.4 collective-permute-start
  990.8 6.4 collective-permute-start
  1048.9 6.4 collective-permute-start
  1107.0 6.4 collective-permute-start
  1165.1 6.4 collective-permute-start
  1223.2 6.4 collective-permute-start
  1281.3 6.4 collective-permute-start
  1339.4 6.4 collective-permute-start
  1397.4 6.4 collective-permute-start
  1455.5 6.4 collective-permute-start
  1513.6 6.4 collective-permute-start
  1571.7 6.4 collective-permute-start
  1578.2 0.7 copy-start.1
Sparse Core Ops, SparseCore 0:
  34.4 93.8 all-reduce.2
  131.3 107.3 all-reduce.4
where the time goes:
time: 1590 us
  blocking collectives  1050 us (66%)
  waiting for transfers between devices  303 us (19%)
  matrix products  117 us (7%)
  starting transfers between devices  44.2 us (3%)
  loops' own time  33.1 us (2%)
  local copies, waits for them, and re-layouts  18.2 us (1%)
    all_gather x23, blocking collectives, tick_step(): part_gain = lax.all_gather(layer_gain, 'tp', axis=1, tiled=True)  519 us
    all_gather x23, blocking collectives, tick_step(): part = lax.all_gather(active, 'tp', axis=1, tiled=True)  504 us
    dot_general x23, matrix products, tick_step(): product = jnp.dot(scaled, weight, preferred_element_type=jnp.float32)  112 us
    psum x1, waiting for transfers between devices, shards(): placed = lax.psum(local_placed, 'section')  108 us
    ppermute x23, waiting for transfers between devices, passed_along(): lax.ppermute(value, axis, [(source, source + steps) for source in range(l...  104 us
    psum x1, waiting for transfers between devices, shards(): total = lax.psum(encoder_terms(whole, vit_gain, vit_up, vit_down), 'tp')  91.4 us
    ppermute x23, starting transfers between devices, passed_along(): lax.ppermute(value, axis, [(source, source + steps) for source in range(l...  44.2 us
    another operation x1, loops' own time, shards(): lax.scan(tick_step, start_carry, jnp.arange(ticks, dtype=jnp.int32))  33.1 us
  transfers between devices with their start and end apart: 25, of which 25 were waited for; matrix products, arithmetic and copies ran while one was open for 0% of the time, Pallas kernels for 0%

commit v1 on v0

v1 whole, which is shorter than its diff:
```python
import functools

import jax
import jax.numpy as jnp
from jax import lax
from jax.experimental import pallas as pl
from jax.experimental.pallas import tpu as pltpu
from jax.sharding import PartitionSpec as P

MESH = pl.DeviceIdType.MESH
F32 = jnp.float32
BF16 = jnp.bfloat16

D = 8192
DV = 1664
POOL = 4
EPSILON = 1e-05
SIDE = 4
TP = SIDE * SIDE
SECTIONS = 16
ROWS = 256
CAP = 16
WIDTH = D // TP
LANES = 128
COLS = DV // LANES
R = 16
STEPS = ROWS // R
AHEAD = 2


def hops(offset):
    return sum(min(o, SIDE - o) for o in offset)


OFFSETS = sorted(((a, b) for a in range(SIDE) for b in range(SIDE)), key=hops)


def slot_at_target(offset):
    return OFFSETS.index(tuple((SIDE - o) % SIDE for o in offset))


def kernel(
    patches,
    vit_gain,
    counts,
    dest,
    layer_gain,
    vit_up,
    vit_down,
    project,
    text,
    weight,
    out,
    up_v,
    down_v,
    project_v,
    text_v,
    weight_v,
    normed,
    partial,
    parts,
    pooled,
    embed_own,
    embeds,
    onehot,
    start,
    gain_own,
    gains,
    features,
    load_sem,
    weight_sem,
    send_sem,
    normed_sem,
    parts_sem,
    pooled_sem,
    gain_sem,
    embed_sem,
    start_send,
    layer_send,
    feature_sem,
):
    section = lax.axis_index("section")
    me = lax.axis_index("tp")
    x, y = me // SIDE, me % SIDE

    def at(offset):
        return (x + offset[0]) % SIDE * SIDE + (y + offset[1]) % SIDE

    loads = [
        pltpu.make_async_copy(source, target, load_sem.at[i])
        for i, (source, target) in enumerate(
            ((vit_up, up_v), (vit_down, down_v), (project, project_v), (text, text_v))
        )
    ]
    for load in loads:
        load.start()
    for i, offset in enumerate(OFFSETS):
        pltpu.make_async_copy(
            weight.at[pl.ds(pl.multiple_of(at(offset) * WIDTH, WIDTH), WIDTH)],
            weight_v.at[i],
            weight_sem,
        ).start()

    barrier = pltpu.get_barrier_semaphore()

    def greet(to_section, to):
        pl.semaphore_signal(barrier, inc=1, device_id=(to_section, to), device_id_type=MESH)

    for offset in OFFSETS[1:]:
        greet(section, at(offset))

    @pl.when(section > 0)
    def _():
        for offset in OFFSETS:
            greet(section - 1, at(offset))

    @pl.when(section == 0)
    def _():
        for other in range(1, SECTIONS):
            greet(other, me)

    values = patches[...].astype(F32)
    centred = values - jnp.mean(values, axis=1, keepdims=True)
    spread = jnp.mean(centred * centred, axis=1, keepdims=True)
    normed[me] = (centred * lax.rsqrt(spread + EPSILON) * vit_gain[...]).astype(BF16)
    residual = jnp.mean(values, axis=0, keepdims=True)
    gain_own[...] = layer_gain[...].astype(F32)
    gains[0] = layer_gain[...].astype(F32)

    peers = TP - 1 + jnp.where(section < SECTIONS - 1, TP, 0) + jnp.where(section > 0, 1, 0)
    pl.semaphore_wait(barrier, peers)

    def send(source, target, recv_sem, to, sem, to_section=section):
        copy = pltpu.make_async_remote_copy(
            src_ref=source,
            dst_ref=target,
            send_sem=sem,
            recv_sem=recv_sem,
            device_id=(to_section, to),
            device_id_type=MESH,
        )
        copy.start()
        return copy

    def arrived(target, sem):
        pltpu.make_async_copy(target, target, sem).wait()

    sent = []
    for i, offset in reversed(list(enumerate(OFFSETS))[1:]):
        sent.append(
            send(normed.at[me], normed.at[me], normed_sem.at[me], at(offset), send_sem.at[0, i])
        )
    for i, offset in reversed(list(enumerate(OFFSETS))[1:]):
        slot = slot_at_target(offset)
        sent.append(
            send(gain_own, gains.at[slot], gain_sem.at[slot], at(offset), send_sem.at[1, i])
        )

    @pl.when(section == 0)
    def _():
        square = (CAP, CAP)
        spots = lax.broadcasted_iota(jnp.int32, square, 1)
        groups = lax.broadcasted_iota(jnp.int32, square, 0)
        limits = jnp.sum(
            jnp.where(spots == groups, counts[...].astype(F32), 0.0), axis=1, keepdims=True
        )
        wanted = jnp.where(spots.astype(F32) < limits, dest[...].astype(F32), -1.0)
        flat = (CAP, SECTIONS * CAP)
        column = lax.broadcasted_iota(jnp.int32, flat, 1)
        line = lax.broadcasted_iota(jnp.int32, flat, 0)
        spread_out = jnp.dot(
            wanted.astype(BF16), (column % CAP == line).astype(BF16), preferred_element_type=F32
        )
        targets = jnp.sum(
            jnp.where(column // CAP == line, spread_out, 0.0), axis=0, keepdims=True
        )
        rows = lax.broadcasted_iota(jnp.int32, (ROWS, SECTIONS * CAP), 0).astype(F32)
        onehot[...] = (rows == targets).astype(BF16)

    loads[0].wait()
    loads[1].wait()
    for offset in OFFSETS[1:]:
        source = at(offset)
        arrived(normed.at[source], normed_sem.at[source])
    whole = normed[...].reshape(TP * POOL, DV)
    hidden = jax.nn.gelu(
        jnp.dot(whole, up_v[...], preferred_element_type=F32), approximate=True
    ).astype(BF16)
    merge = lax.broadcasted_iota(jnp.int32, (TP, TP * POOL), 1) // POOL == lax.broadcasted_iota(
        jnp.int32, (TP, TP * POOL), 0
    )
    merged = jnp.dot(
        jnp.where(merge, 1.0 / POOL, 0.0).astype(BF16), hidden, preferred_element_type=F32
    )
    terms = jnp.dot(merged.astype(BF16), down_v[...], preferred_element_type=F32)
    mine = lax.broadcasted_iota(jnp.int32, (TP, DV), 0) == me
    terms = (terms + jnp.where(mine, residual, 0.0)).astype(BF16)
    for j in range(COLS):
        partial[j] = terms[:, j * LANES : (j + 1) * LANES]

    for i, offset in reversed(list(enumerate(OFFSETS))[1:]):
        to = at(offset)

        @pl.when(to < COLS)
        def _():
            send(partial.at[to], parts.at[me], parts_sem.at[me], to, send_sem.at[2, i])

    @pl.when(me < COLS)
    def _():
        parts[me] = partial[me]
        for offset in OFFSETS[1:]:
            source = at(offset)
            arrived(parts.at[source], parts_sem.at[source])
        total = jnp.sum(parts[...].astype(F32), axis=0)
        block = pl.ds(pl.multiple_of(me * LANES, LANES), LANES)
        pooled[:, block] = total.astype(BF16)
        for i, offset in reversed(list(enumerate(OFFSETS))[1:]):
            send(
                pooled.at[:, block],
                pooled.at[:, block],
                pooled_sem.at[me],
                at(offset),
                send_sem.at[3, i],
            )

    loads[2].wait()
    for offset in OFFSETS[1:]:
        source = at(offset)

        @pl.when(source < COLS)
        def _():
            block = pl.ds(pl.multiple_of(source * LANES, LANES), LANES)
            arrived(pooled.at[:, block], pooled_sem.at[source])

    embed = jnp.dot(pooled[...], project_v[...], preferred_element_type=F32).astype(BF16)

    @pl.when(section > 0)
    def _():
        embed_own[...] = embed
        send(embed_own, embeds.at[section], embed_sem.at[section], me, send_sem.at[4, 0], 0)

    loads[3].wait()

    def start_rows(m):
        rows = pl.ds(pl.multiple_of(m * R, R), R)
        placed = jnp.dot(
            onehot[rows, :],
            embeds[...].reshape(SECTIONS * CAP, WIDTH),
            preferred_element_type=F32,
        )
        first = (text_v[rows, :].astype(F32) + placed).astype(BF16)
        start[rows, :] = first
        features[m, 0] = first
        for offset in reversed(OFFSETS[1:]):
            slot = slot_at_target(offset)
            send(
                start.at[rows, :],
                features.at[m, slot],
                feature_sem.at[m, slot],
                at(offset),
                start_send.at[m],
            )

    @pl.when(section == 0)
    def _():
        embeds[0] = embed
        for other in range(1, SECTIONS):
            arrived(embeds.at[other], embed_sem.at[other])
        for m in range(AHEAD):
            start_rows(m)

    for i in range(1, TP):
        arrived(gains.at[i], gain_sem.at[i])
    arrived(weight_v, weight_sem)

    def step(m, carry):
        @pl.when((section == 0) & (m + AHEAD < STEPS))
        def _():
            start_rows(m + AHEAD)

        @pl.when(section > 0)
        def _():
            arrived(features.at[m, 0], feature_sem.at[m, 0])

        product = jnp.zeros((R, WIDTH), F32)
        squares = jnp.zeros((R, LANES), F32)
        for i in range(TP):
            if i:
                arrived(features.at[m, i], feature_sem.at[m, i])
            part = features[m, i].astype(F32)
            for c in range(0, WIDTH, LANES):
                squares += part[:, c : c + LANES] * part[:, c : c + LANES]
            scaled = (part * gains[i]).astype(BF16)
            product += jnp.dot(scaled, weight_v[i], preferred_element_type=F32)
        scale = lax.rsqrt(jnp.sum(squares, axis=1, keepdims=True) / D + EPSILON)
        rows = pl.ds(pl.multiple_of(m * R, R), R)
        out[rows, :] = (features[m, 0].astype(F32) + product * scale).astype(BF16)

        @pl.when(section < SECTIONS - 1)
        def _():
            for offset in reversed(OFFSETS):
                slot = slot_at_target(offset)
                send(
                    out.at[rows, :],
                    features.at[m, slot],
                    feature_sem.at[m, slot],
                    at(offset),
                    layer_send.at[m],
                    section + 1,
                )

        return carry

    lax.fori_loop(0, STEPS, step, 0)

    for copy in sent:
        copy.wait_send()
    for i, offset in list(enumerate(OFFSETS))[1:]:
        to = at(offset)

        @pl.when(to < COLS)
        def _():
            arrived(partial.at[0], send_sem.at[2, i])

        @pl.when(me < COLS)
        def _():
            arrived(partial.at[0], send_sem.at[3, i])

    @pl.when(section > 0)
    def _():
        arrived(embed_own, send_sem.at[4, 0])

    def drain(m, carry):
        @pl.when(section == 0)
        def _():
            arrived(features.at[m, pl.ds(0, TP - 1)], start_send.at[m])

        @pl.when(section < SECTIONS - 1)
        def _():
            arrived(features.at[m], layer_send.at[m])

        return carry

    lax.fori_loop(0, STEPS, drain, 0)


def shards(
    patches,
    vit_gain,
    vit_up,
    vit_down,
    project,
    text,
    image_counts,
    image_dest,
    layer_gain,
    layer_weight,
):
    vmem = pl.BlockSpec(memory_space=pltpu.VMEM)
    anywhere = pl.BlockSpec(memory_space=pl.ANY)
    dma = pltpu.SemaphoreType.DMA
    hidden = vit_up.shape[1]
    outputs = pl.pallas_call(
        kernel,
        out_shape=jax.ShapeDtypeStruct((ROWS, WIDTH), BF16),
        in_specs=[vmem] * 5 + [anywhere] * 5,
        out_specs=vmem,
        scratch_shapes=[
            pltpu.VMEM((DV, hidden), BF16),
            pltpu.VMEM((hidden, DV), BF16),
            pltpu.VMEM((DV, WIDTH), BF16),
            pltpu.VMEM((ROWS, WIDTH), BF16),
            pltpu.VMEM((TP, WIDTH, WIDTH), BF16),
            pltpu.VMEM((TP, POOL, DV), BF16),
            pltpu.VMEM((COLS, TP, LANES), BF16),
            pltpu.VMEM((TP, TP, LANES), BF16),
            pltpu.VMEM((TP, DV), BF16),
            pltpu.VMEM((CAP, WIDTH), BF16),
            pltpu.VMEM((SECTIONS, CAP, WIDTH), BF16),
            pltpu.VMEM((ROWS, SECTIONS * CAP), BF16),
            pltpu.VMEM((ROWS, WIDTH), BF16),
            pltpu.VMEM((1, WIDTH), F32),
            pltpu.VMEM((TP, 1, WIDTH), F32),
            pltpu.VMEM((STEPS, TP, R, WIDTH), BF16),
            dma((4,)),
            dma,
            dma((5, TP)),
            dma((TP,)),
            dma((TP,)),
            dma((TP,)),
            dma((TP,)),
            dma((SECTIONS,)),
            dma((STEPS,)),
            dma((STEPS,)),
            dma((STEPS, TP)),
        ],
        compiler_params=pltpu.CompilerParams(
            collective_id=0, has_side_effects=True, vmem_limit_bytes=40 << 20
        ),
        cost_estimate=pl.CostEstimate(
            flops=2 * ROWS * D * WIDTH, bytes_accessed=12 << 20, transcendentals=0
        ),
        name="encoder_and_layers",
    )(
        patches,
        vit_gain[None],
        image_counts[None],
        image_dest,
        layer_gain,
        vit_up,
        vit_down,
        project,
        text,
        layer_weight[0],
    )
    return outputs.reshape(1, 8, ROWS // 8, WIDTH)


def solution(mesh):
    in_specs = (
        P(("section", "tp"), None),
        P(),
        P(None, "tp"),
        P("tp", None),
        P(None, "tp"),
        P(None, "tp"),
        P(),
        P(),
        P("section", "tp"),
        P("section", None, "tp"),
    )
    out_specs = P("section", None, None, "tp")
    return jax.shard_map(shards, mesh=mesh, in_specs=in_specs, out_specs=out_specs, check_vma=False)
```

time: 1590 us -> 201 us (0.13)
  the two profiles are of different devices: /device:TPU:128 before, /device:TPU:225 now
where the time goes in v1:
time: 201 us; the launch traced here: 200 us
  Pallas kernels  188 us (94%)
  local copies, waits for them, and re-layouts  12.2 us (6%)
    pallas_call x1, Pallas kernels, shards(): pl.pallas_call(kernel, out_shape=jax.ShapeDtypeStruct((ROWS, WIDTH), BF16...  188 us
    unnamed x19, local copies, waits for them, and re-layouts  11.5 us

profile of v1, /device:TPU:225, one launch (start us, length us, event | category | flops | bytes accessed | tf_op | source)
XLA Modules:
  0.0 200.5 jit_solution(3594367990053695749)
XLA Ops:
  0.0 0.7 broadcast_in_dim.6.vit_gain
  0.7 0.0 copy-start
  0.7 3.4 %copy-done = bf16[1,8192,512]{2,1,0:T(8,128)(2,1)S(1)} copy-done((bf16[1,8192,512]{2,1,0:T(8,128)(2,1)S(1)}, bf16[1,8192,512]{2,1,0:T(8,128)(2,1)}, u32[]{:S(2)}) %copy-start) | copy-done | bytes 8388632
  4.1 0.0 copy-start.1
  4.1 1.5 copy-done.1
  5.5 0.0 copy-start.2
  5.5 1.2 copy-done.2
  6.7 0.0 copy-start.3
  6.7 1.2 copy-done.3
  7.9 0.0 copy-start.4
  7.9 0.9 copy-done.4
  8.8 0.0 copy-start.5
  8.8 0.7 copy-done.5
  9.5 0.0 copy-start.6
  9.5 0.7 copy-done.6
  10.2 0.0 copy-start.7
  10.2 0.7 copy-done.7
  10.9 0.0 copy-start.8
  10.9 0.7 copy-done.8
  11.5 188.2 %encoder_and_layers.1 = bf16[256,512]{1,0:T(8,128)(2,1)S(1)} custom-call(bf16[4,1664]{1,0:T(4,128)(2,1)S(1)} %copy-done.5, f32[1,1664]{1,0:T(1,128)S(1)} %broadcast_in_dim.6.vit_gain, s32[1,16]{1,0:T(1,128)S(1)} %bitcast.5, s32[16,16]{1,0:T(8,128)S(1)} %copy-done.6, bf16[1,512]{1,0:T(2,128)(2,1)S(1)} %copy-done.7, bf16[1664,256]{1,0:T(8,128)(2,1)S(1)} %copy-done.2, ...), custom_call_target="tpu_custom_call" | custom-call | flops 2147483648 | bytes 12582912 | tf_op jit(solution)/shard_map/encoder_and_layers/pallas_call | solution.py:363
  199.8 0.7 copy.12
Async XLA Ops:
  0.7 3.4 %copy-start = (bf16[1,8192,512]{2,1,0:T(8,128)(2,1)S(1)}, bf16[1,8192,512]{2,1,0:T(8,128)(2,1)}, u32[]{:S(2)}) copy-start(bf16[1,8192,512]{2,1,0:T(8,128)(2,1)} %param.19) | copy-start | bytes 25165828
  4.1 1.5 copy-start.1
  5.5 1.2 copy-start.2
  6.7 1.2 copy-start.3
  7.9 0.9 copy-start.4
  8.8 0.7 copy-start.5
  9.5 0.7 copy-start.6
  10.2 0.7 copy-start.7
  10.9 0.7 copy-start.8

commit v2 on v1

--- a/solution.py
+++ b/solution.py
@@ -40,17 +40,22 @@
 
 
 def kernel(
-    patches,
-    vit_gain,
-    counts,
-    dest,
-    layer_gain,
+    patches_in,
+    vit_gain_in,
+    counts_in,
+    dest_in,
+    layer_gain_in,
     vit_up,
     vit_down,
     project,
     text,
     weight,
     out,
+    patches,
+    vit_gain,
+    counts,
+    dest,
+    layer_gain,
     up_v,
     down_v,
     project_v,
@@ -89,7 +94,17 @@
     loads = [
         pltpu.make_async_copy(source, target, load_sem.at[i])
         for i, (source, target) in enumerate(
-            ((vit_up, up_v), (vit_down, down_v), (project, project_v), (text, text_v))
+            (
+                (patches_in, patches),
+                (vit_gain_in, vit_gain),
+                (layer_gain_in, layer_gain),
+                (counts_in, counts),
+                (dest_in, dest),
+                (vit_up, up_v),
+                (vit_down, down_v),
+                (project, project_v),
+                (text, text_v),
+            )
         )
     ]
     for load in loads:
@@ -119,10 +134,12 @@
         for other in range(1, SECTIONS):
             greet(other, me)
 
+    for load in loads[:3]:
+        load.wait()
     values = patches[...].astype(F32)
     centred = values - jnp.mean(values, axis=1, keepdims=True)
     spread = jnp.mean(centred * centred, axis=1, keepdims=True)
-    normed[me] = (centred * lax.rsqrt(spread + EPSILON) * vit_gain[...]).astype(BF16)
+    normed[me] = (centred * lax.rsqrt(spread + EPSILON) * vit_gain[...][None]).astype(BF16)
     residual = jnp.mean(values, axis=0, keepdims=True)
     gain_own[...] = layer_gain[...].astype(F32)
     gains[0] = layer_gain[...].astype(F32)
@@ -156,13 +173,16 @@
             send(gain_own, gains.at[slot], gain_sem.at[slot], at(offset), send_sem.at[1, i])
         )
 
+    loads[3].wait()
+    loads[4].wait()
+
     @pl.when(section == 0)
     def _():
         square = (CAP, CAP)
         spots = lax.broadcasted_iota(jnp.int32, square, 1)
         groups = lax.broadcasted_iota(jnp.int32, square, 0)
         limits = jnp.sum(
-            jnp.where(spots == groups, counts[...].astype(F32), 0.0), axis=1, keepdims=True
+            jnp.where(spots == groups, counts[...][None].astype(F32), 0.0), axis=1, keepdims=True
         )
         wanted = jnp.where(spots.astype(F32) < limits, dest[...].astype(F32), -1.0)
         flat = (CAP, SECTIONS * CAP)
@@ -177,8 +197,8 @@
         rows = lax.broadcasted_iota(jnp.int32, (ROWS, SECTIONS * CAP), 0).astype(F32)
         onehot[...] = (rows == targets).astype(BF16)
 
-    loads[0].wait()
-    loads[1].wait()
+    loads[5].wait()
+    loads[6].wait()
     for offset in OFFSETS[1:]:
         source = at(offset)
         arrived(normed.at[source], normed_sem.at[source])
@@ -223,7 +243,7 @@
                 send_sem.at[3, i],
             )
 
-    loads[2].wait()
+    loads[7].wait()
     for offset in OFFSETS[1:]:
         source = at(offset)
 
@@ -239,7 +259,7 @@
         embed_own[...] = embed
         send(embed_own, embeds.at[section], embed_sem.at[section], me, send_sem.at[4, 0], 0)
 
-    loads[3].wait()
+    loads[8].wait()
 
     def start_rows(m):
         rows = pl.ds(pl.multiple_of(m * R, R), R)
@@ -357,15 +377,20 @@
     layer_weight,
 ):
     vmem = pl.BlockSpec(memory_space=pltpu.VMEM)
-    anywhere = pl.BlockSpec(memory_space=pl.ANY)
+    hbm = pl.BlockSpec(memory_space=pltpu.HBM)
     dma = pltpu.SemaphoreType.DMA
     hidden = vit_up.shape[1]
     outputs = pl.pallas_call(
         kernel,
         out_shape=jax.ShapeDtypeStruct((ROWS, WIDTH), BF16),
-        in_specs=[vmem] * 5 + [anywhere] * 5,
+        in_specs=[hbm] * 10,
         out_specs=vmem,
         scratch_shapes=[
+            pltpu.VMEM(patches.shape, BF16),
+            pltpu.VMEM(vit_gain.shape, F32),
+            pltpu.VMEM(image_counts.shape, jnp.int32),
+            pltpu.VMEM(image_dest.shape, jnp.int32),
+            pltpu.VMEM(layer_gain.shape, BF16),
             pltpu.VMEM((DV, hidden), BF16),
             pltpu.VMEM((hidden, DV), BF16),
             pltpu.VMEM((DV, WIDTH), BF16),
@@ -382,7 +407,7 @@
             pltpu.VMEM((1, WIDTH), F32),
             pltpu.VMEM((TP, 1, WIDTH), F32),
             pltpu.VMEM((STEPS, TP, R, WIDTH), BF16),
-            dma((4,)),
+            dma((9,)),
             dma,
             dma((5, TP)),
             dma((TP,)),
@@ -395,7 +420,7 @@
             dma((STEPS, TP)),
         ],
         compiler_params=pltpu.CompilerParams(
-            collective_id=0, has_side_effects=True, vmem_limit_bytes=40 << 20
+            collective_id=0, has_side_effects=True, vmem_limit_bytes=60 << 20
         ),
         cost_estimate=pl.CostEstimate(
             flops=2 * ROWS * D * WIDTH, bytes_accessed=12 << 20, transcendentals=0
@@ -403,8 +428,8 @@
         name="encoder_and_layers",
     )(
         patches,
-        vit_gain[None],
-        image_counts[None],
+        vit_gain,
+        image_counts,
         image_dest,
         layer_gain,
         vit_up,

time: 201 us -> 188 us (0.935)
  local copies, waits for them, and re-layouts: 12.2 us -> 1.67 us
    unnamed x19 -> x1, local copies, waits for them, and re-layouts: 11.5 us -> 1.67 us
where the time goes in v2:
time: 188 us
  Pallas kernels  187 us (99%)
    pallas_call x1, Pallas kernels, shards(): pl.pallas_call(kernel, out_shape=jax.ShapeDtypeStruct((ROWS, WIDTH), BF16...  187 us

profile of v2, /device:TPU:225, one launch (start us, length us, event | category | flops | bytes accessed | tf_op | source)
XLA Modules:
  0.0 188.3 jit_solution(3164690699774723607)
XLA Ops:
  0.0 186.6 %encoder_and_layers.1 = bf16[256,512]{1,0:T(8,128)(2,1)} custom-call(bf16[4,1664]{1,0:T(4,128)(2,1)} %patches_in.1, f32[1664]{0:T(1024)} %vit_gain_in.1, s32[16]{0:T(128)} %counts_in.1, s32[16,16]{1,0:T(8,128)} %dest_in.1, bf16[1,512]{1,0:T(2,128)(2,1)} %layer_gain_in.1, bf16[1664,256]{1,0:T(8,128)(2,1)} %vit_up.1, bf16[256,1664]{1,0:T(8,128)(2,1)} %vit_down.1, ...), custom_call_target="tpu_custom_call" | custom-call | flops 2147483648 | bytes 12582912 | tf_op jit(solution)/shard_map/encoder_and_layers/pallas_call | solution.py:383
  186.6 1.7 copy.12

commit v3 on v2

v3 whole, which is shorter than its diff:
```python
import functools

import jax
import jax.numpy as jnp
from jax import lax
from jax.experimental import pallas as pl
from jax.experimental.pallas import tpu as pltpu
from jax.sharding import PartitionSpec as P

MESH = pl.DeviceIdType.MESH
F32 = jnp.float32
BF16 = jnp.bfloat16

D = 8192
DV = 1664
POOL = 4
EPSILON = 1e-05
SIDE = 4
TP = SIDE * SIDE
SECTIONS = 16
ROWS = 256
CAP = 16
WIDTH = D // TP
LANES = 128
COLS = DV // LANES
R = 8
STEPS = ROWS // R
PAIRS = STEPS // 2
AHEAD = 2
BATCHES = 4


def hops(offset):
    return sum(min(o, SIDE - o) for o in offset)


OFFSETS = sorted(((a, b) for a in range(SIDE) for b in range(SIDE)), key=hops)
FAR_FIRST = list(reversed(list(enumerate(OFFSETS))))
CLASSES = [
    (lo, lo + sum(hops(o) == h for o in OFFSETS))
    for h, lo in [(hops(o), i) for i, o in enumerate(OFFSETS) if i == 0 or hops(o) != hops(OFFSETS[i - 1])]
]


def slot_at_target(offset):
    return OFFSETS.index(tuple((SIDE - o) % SIDE for o in offset))


def kernel(
    patches_in,
    vit_gain_in,
    counts_in,
    dest_in,
    layer_gain_in,
    vit_up,
    vit_down,
    project,
    text,
    weight,
    out,
    patches,
    vit_gain,
    counts,
    dest,
    layer_gain,
    up_v,
    down_v,
    project_v,
    text_v,
    weight_v,
    normed,
    partial,
    parts,
    pooled,
    embed_own,
    embeds,
    onehot,
    start,
    gain_own,
    gains,
    features,
    result,
    load_sem,
    weight_sem,
    phase_send,
    phase_recv,
    start_send,
    layer_send,
    feature_sem,
    out_sem,
):
    section = lax.axis_index("section")
    me = lax.axis_index("tp")
    x, y = me // SIDE, lax.rem(me, SIDE)
    targets = [
        lax.rem(x + offset[0], SIDE) * SIDE + lax.rem(y + offset[1], SIDE) for offset in OFFSETS
    ]
    peers = [(i, targets[i]) for i, _ in FAR_FIRST if i]

    barrier = pltpu.get_barrier_semaphore()

    def greet(to_section, to):
        pl.semaphore_signal(barrier, inc=1, device_id=(to_section, to), device_id_type=MESH)

    for _, to in peers:
        greet(section, to)

    @pl.when(section == 0)
    def _():
        for other in range(1, SECTIONS):
            greet(other, me)

    @pl.when(section > 0)
    def _():
        for i, _ in FAR_FIRST:
            greet(section - 1, targets[i])

    loads = [
        pltpu.make_async_copy(source, target, load_sem.at[i])
        for i, (source, target) in enumerate(
            (
                (patches_in, patches),
                (vit_gain_in, vit_gain),
                (layer_gain_in, layer_gain),
                (counts_in, counts),
                (dest_in, dest),
                (vit_up, up_v),
                (vit_down, down_v),
                (project, project_v),
                (text, text_v),
            )
        )
    ]
    for load in loads:
        load.start()
    for i in range(TP):
        pltpu.make_async_copy(
            weight.at[pl.ds(pl.multiple_of(targets[i] * WIDTH, WIDTH), WIDTH)],
            weight_v.at[i],
            weight_sem,
        ).start()

    for load in loads[:3]:
        load.wait()
    values = patches[...].astype(F32)
    centred = values - jnp.mean(values, axis=1, keepdims=True)
    spread = jnp.mean(centred * centred, axis=1, keepdims=True)
    normed[me] = (centred * lax.rsqrt(spread + EPSILON) * vit_gain[...][None]).astype(BF16)
    residual = jnp.mean(values, axis=0, keepdims=True)
    gain_own[...] = layer_gain[...].astype(F32)
    gains[0] = layer_gain[...].astype(F32)

    greeted = TP - 1 + jnp.where(section < SECTIONS - 1, TP, 0) + jnp.where(section > 0, 1, 0)
    pl.semaphore_wait(barrier, greeted)

    def send(source, target, recv_sem, to, sem, to_section=section):
        pltpu.make_async_remote_copy(
            src_ref=source,
            dst_ref=target,
            send_sem=sem,
            recv_sem=recv_sem,
            device_id=(to_section, to),
            device_id_type=MESH,
        ).start()

    def arrived(target, sem):
        pltpu.make_async_copy(target, target, sem).wait()

    for _, to in peers:
        send(normed.at[me], normed.at[me], phase_recv.at[0], to, phase_send.at[0])
    for i, to in peers:
        slot = slot_at_target(OFFSETS[i])
        send(gain_own, gains.at[slot], phase_recv.at[1], to, phase_send.at[1])

    loads[3].wait()
    loads[4].wait()

    @pl.when(section == 0)
    def _():
        square = (CAP, CAP)
        spots = lax.broadcasted_iota(jnp.int32, square, 1)
        groups = lax.broadcasted_iota(jnp.int32, square, 0)
        limits = jnp.sum(
            jnp.where(spots == groups, counts[...][None].astype(F32), 0.0), axis=1, keepdims=True
        )
        wanted = jnp.where(spots.astype(F32) < limits, dest[...].astype(F32), -1.0)
        flat = (CAP, SECTIONS * CAP)
        column = lax.broadcasted_iota(jnp.int32, flat, 1)
        line = lax.broadcasted_iota(jnp.int32, flat, 0)
        spread_out = jnp.dot(
            wanted.astype(BF16), (column % CAP == line).astype(BF16), preferred_element_type=F32
        )
        places = jnp.sum(jnp.where(column // CAP == line, spread_out, 0.0), axis=0, keepdims=True)
        rows = lax.broadcasted_iota(jnp.int32, (ROWS, SECTIONS * CAP), 0).astype(F32)
        onehot[...] = (rows == places).astype(BF16)

    loads[5].wait()
    loads[6].wait()
    arrived(normed.at[pl.ds(0, TP - 1)], phase_recv.at[0])
    whole = normed[...].reshape(TP * POOL, DV)
    hidden = jax.nn.gelu(
        jnp.dot(whole, up_v[...], preferred_element_type=F32), approximate=True
    ).astype(BF16)
    merge = lax.broadcasted_iota(jnp.int32, (TP, TP * POOL), 1) // POOL == lax.broadcasted_iota(
        jnp.int32, (TP, TP * POOL), 0
    )
    merged = jnp.dot(
        jnp.where(merge, 1.0 / POOL, 0.0).astype(BF16), hidden, preferred_element_type=F32
    )
    terms = jnp.dot(merged.astype(BF16), down_v[...], preferred_element_type=F32)
    mine = lax.broadcasted_iota(jnp.int32, (TP, DV), 0) == me
    terms = (terms + jnp.where(mine, residual, 0.0)).astype(BF16)
    for j in range(COLS):
        partial[j] = terms[:, j * LANES : (j + 1) * LANES]

    for i, to in peers:

        @pl.when(to < COLS)
        def _():
            send(partial.at[to], parts.at[me], phase_recv.at[2], to, phase_send.at[2])

    @pl.when(me < COLS)
    def _():
        parts[me] = partial[me]
        arrived(parts.at[pl.ds(0, TP - 1)], phase_recv.at[2])
        total = jnp.sum(parts[...].astype(F32), axis=0)
        block = pl.ds(pl.multiple_of(me * LANES, LANES), LANES)
        pooled[:, block] = total.astype(BF16)
        for _, to in peers:
            send(pooled.at[:, block], pooled.at[:, block], phase_recv.at[3], to, phase_send.at[3])
        arrived(pooled.at[:, pl.ds(0, (COLS - 1) * LANES)], phase_recv.at[3])

    @pl.when(me >= COLS)
    def _():
        arrived(pooled, phase_recv.at[3])

    loads[7].wait()
    embed = jnp.dot(pooled[...], project_v[...], preferred_element_type=F32).astype(BF16)

    @pl.when(section > 0)
    def _():
        embed_own[...] = embed
        send(embed_own, embeds.at[section], phase_recv.at[4], me, phase_send.at[4], 0)

    loads[8].wait()

    def spread_rows(p):
        two = pl.ds(2 * p, 2)
        features[two, 0] = start[two]
        for i, to in peers:
            slot = slot_at_target(OFFSETS[i])
            (c,) = [c for c, (lo, hi) in enumerate(CLASSES) if lo <= slot < hi]
            send(
                start.at[two],
                features.at[two, slot],
                feature_sem.at[2 * p, c],
                to,
                start_send.at[2 * p * BATCHES // STEPS],
            )

    @pl.when(section == 0)
    def _():
        embeds[0] = embed
        arrived(embeds.at[pl.ds(0, SECTIONS - 1)], phase_recv.at[4])
        for p in range(PAIRS):
            rows = slice(2 * R * p, 2 * R * (p + 1))
            placed = jnp.dot(
                onehot[rows, :],
                embeds[...].reshape(SECTIONS * CAP, WIDTH),
                preferred_element_type=F32,
            )
            first = text_v[rows, :].astype(F32) + placed
            start[2 * p : 2 * p + 2] = first.reshape(2, R, WIDTH).astype(BF16)
            if p < AHEAD:
                spread_rows(p)

    arrived(gains.at[pl.ds(0, TP - 1)], phase_recv.at[1])
    arrived(weight_v, weight_sem)

    def layer(m, wait):
        product = jnp.zeros((R, WIDTH), F32)
        squares = jnp.zeros((R, LANES), F32)
        for c, (lo, hi) in enumerate(CLASSES):
            wait(c, pl.ds(lo, hi - lo))
            for i in range(lo, hi):
                part = features[m, i].astype(F32)
                for at in range(0, WIDTH, LANES):
                    squares += part[:, at : at + LANES] * part[:, at : at + LANES]
                scaled = (part * gains[i]).astype(BF16)
                product += jnp.dot(scaled, weight_v[i], preferred_element_type=F32)
        scale = lax.rsqrt(jnp.sum(squares, axis=1, keepdims=True) / D + EPSILON)
        result[m] = (features[m, 0].astype(F32) + product * scale).astype(BF16)

    def hand_on(m):
        for i, offset in FAR_FIRST:
            slot = slot_at_target(offset)
            (c,) = [c for c, (lo, hi) in enumerate(CLASSES) if lo <= slot < hi]
            send(
                result.at[m],
                features.at[m, slot],
                feature_sem.at[m, c],
                targets[i],
                layer_send.at[m * BATCHES // STEPS],
                section + 1,
            )

    def store(p):
        two = pl.ds(2 * p, 2)
        pltpu.make_async_copy(result.at[two], out.at[two], out_sem).start()

    @pl.when(section == 0)
    def _():
        def pair(p, carry):
            @pl.when(p + AHEAD < PAIRS)
            def _():
                spread_rows(p + AHEAD)

            def wait(c, slots):
                if c:
                    arrived(features.at[pl.ds(2 * p, 2), slots], feature_sem.at[2 * p, c])

            layer(2 * p, wait)
            hand_on(2 * p)
            layer(2 * p + 1, lambda c, slots: None)
            hand_on(2 * p + 1)
            store(p)
            return carry

        lax.fori_loop(0, PAIRS, pair, 0)

    @pl.when(section > 0)
    def _():
        def pair(p, carry):
            for m in (2 * p, 2 * p + 1):
                layer(m, lambda c, slots: arrived(features.at[m, slots], feature_sem.at[m, c]))

                @pl.when(section < SECTIONS - 1)
                def _():
                    hand_on(m)

            store(p)
            return carry

        lax.fori_loop(0, PAIRS, pair, 0)

    arrived(normed.at[pl.ds(0, TP - 1)], phase_send.at[0])
    arrived(gains.at[pl.ds(0, TP - 1)], phase_send.at[1])

    @pl.when(me < COLS)
    def _():
        arrived(partial.at[pl.ds(0, COLS - 1)], phase_send.at[2])
        arrived(parts.at[pl.ds(0, TP - 1)], phase_send.at[3])

    @pl.when(me >= COLS)
    def _():
        arrived(partial, phase_send.at[2])

    @pl.when(section > 0)
    def _():
        arrived(embed_own, phase_send.at[4])

    many = STEPS // BATCHES

    @pl.when(section == 0)
    def _():
        for b in range(BATCHES):
            arrived(features.at[pl.ds(b * many, many), pl.ds(0, TP - 1)], start_send.at[b])

    @pl.when(section < SECTIONS - 1)
    def _():
        for b in range(BATCHES):
            arrived(features.at[pl.ds(b * many, many)], layer_send.at[b])

    arrived(result, out_sem)


def shards(
    patches,
    vit_gain,
    vit_up,
    vit_down,
    project,
    text,
    image_counts,
    image_dest,
    layer_gain,
    layer_weight,
):
    hbm = pl.BlockSpec(memory_space=pltpu.HBM)
    dma = pltpu.SemaphoreType.DMA
    hidden = vit_up.shape[1]
    outputs = pl.pallas_call(
        kernel,
        out_shape=jax.ShapeDtypeStruct((STEPS, R, WIDTH), BF16),
        in_specs=[hbm] * 10,
        out_specs=hbm,
        scratch_shapes=[
            pltpu.VMEM(patches.shape, BF16),
            pltpu.VMEM(vit_gain.shape, F32),
            pltpu.VMEM(image_counts.shape, jnp.int32),
            pltpu.VMEM(image_dest.shape, jnp.int32),
            pltpu.VMEM(layer_gain.shape, BF16),
            pltpu.VMEM((DV, hidden), BF16),
            pltpu.VMEM((hidden, DV), BF16),
            pltpu.VMEM((DV, WIDTH), BF16),
            pltpu.VMEM((ROWS, WIDTH), BF16),
            pltpu.VMEM((TP, WIDTH, WIDTH), BF16),
            pltpu.VMEM((TP, POOL, DV), BF16),
            pltpu.VMEM((COLS, TP, LANES), BF16),
            pltpu.VMEM((TP, TP, LANES), BF16),
            pltpu.VMEM((TP, DV), BF16),
            pltpu.VMEM((CAP, WIDTH), BF16),
            pltpu.VMEM((SECTIONS, CAP, WIDTH), BF16),
            pltpu.VMEM((ROWS, SECTIONS * CAP), BF16),
            pltpu.VMEM((STEPS, R, WIDTH), BF16),
            pltpu.VMEM((1, WIDTH), F32),
            pltpu.VMEM((TP, 1, WIDTH), F32),
            pltpu.VMEM((STEPS, TP, R, WIDTH), BF16),
            pltpu.VMEM((STEPS, R, WIDTH), BF16),
            dma((9,)),
            dma,
            dma((5,)),
            dma((5,)),
            dma((BATCHES,)),
            dma((BATCHES,)),
            dma((STEPS, len(CLASSES))),
            dma,
        ],
        compiler_params=pltpu.CompilerParams(
            collective_id=0, has_side_effects=True, vmem_limit_bytes=60 << 20
        ),
        cost_estimate=pl.CostEstimate(
            flops=2 * ROWS * D * WIDTH, bytes_accessed=12 << 20, transcendentals=0
        ),
        name="encoder_and_layers",
    )(
        patches,
        vit_gain,
        image_counts,
        image_dest,
        layer_gain,
        vit_up,
        vit_down,
        project,
        text,
        layer_weight[0],
    )
    return outputs.reshape(1, 8, ROWS // 8, WIDTH)


def solution(mesh):
    in_specs = (
        P(("section", "tp"), None),
        P(),
        P(None, "tp"),
        P("tp", None),
        P(None, "tp"),
        P(None, "tp"),
        P(),
        P(),
        P("section", "tp"),
        P("section", None, "tp"),
    )
    out_specs = P("section", None, None, "tp")
    return jax.shard_map(shards, mesh=mesh, in_specs=in_specs, out_specs=out_specs, check_vma=False)
```

time: 188 us -> 170 us (0.904)
  Pallas kernels: 187 us -> 168 us
    pallas_call x1, Pallas kernels: 187 us -> 168 us  [shards(): pl.pallas_call(kernel, out_shape=jax.ShapeDtypeStruct((STEPS, R, WIDTH),...]
where the time goes in v3:
time: 170 us; the launch traced here: 169 us
  Pallas kernels  168 us (99%)
    pallas_call x1, Pallas kernels, shards(): pl.pallas_call(kernel, out_shape=jax.ShapeDtypeStruct((STEPS, R, WIDTH),...  168 us

profile of v3, /device:TPU:225, one launch (start us, length us, event | category | flops | bytes accessed | tf_op | source)
XLA Modules:
  0.0 169.4 jit_solution(7109505709507068371)
XLA Ops:
  0.0 167.8 %encoder_and_layers.1 = bf16[32,8,512]{2,1,0:T(8,128)(2,1)} custom-call(bf16[4,1664]{1,0:T(4,128)(2,1)} %patches_in.1, f32[1664]{0:T(1024)} %vit_gain_in.1, s32[16]{0:T(128)} %counts_in.1, s32[16,16]{1,0:T(8,128)} %dest_in.1, bf16[1,512]{1,0:T(2,128)(2,1)} %layer_gain_in.1, bf16[1664,256]{1,0:T(8,128)(2,1)} %vit_up.1, bf16[256,1664]{1,0:T(8,128)(2,1)} %vit_down.1, ...), custom_call_target="tpu_custom_call" | custom-call | flops 2147483648 | bytes 12582912 | tf_op jit(solution)/shard_map/encoder_and_layers/pallas_call | solution.py:392
  167.8 1.7 copy.12

commit v4 on v3

--- a/solution.py
+++ b/solution.py
@@ -26,7 +26,7 @@
 R = 8
 STEPS = ROWS // R
 PAIRS = STEPS // 2
-AHEAD = 2
+HALF = TP // 2
 BATCHES = 4
 
 
@@ -72,14 +72,13 @@
     partial,
     parts,
     pooled,
-    embed_own,
-    embeds,
+    start,
     onehot,
-    start,
     gain_own,
     gains,
     features,
     result,
+    ordered,
     load_sem,
     weight_sem,
     phase_send,
@@ -88,6 +87,7 @@
     layer_send,
     feature_sem,
     out_sem,
+    token,
 ):
     section = lax.axis_index("section")
     me = lax.axis_index("tp")
@@ -104,11 +104,6 @@
 
     for _, to in peers:
         greet(section, to)
-
-    @pl.when(section == 0)
-    def _():
-        for other in range(1, SECTIONS):
-            greet(other, me)
 
     @pl.when(section > 0)
     def _():
@@ -150,8 +145,7 @@
     gain_own[...] = layer_gain[...].astype(F32)
     gains[0] = layer_gain[...].astype(F32)
 
-    greeted = TP - 1 + jnp.where(section < SECTIONS - 1, TP, 0) + jnp.where(section > 0, 1, 0)
-    pl.semaphore_wait(barrier, greeted)
+    pl.semaphore_wait(barrier, TP - 1 + jnp.where(section < SECTIONS - 1, TP, 0))
 
     def send(source, target, recv_sem, to, sem, to_section=section):
         pltpu.make_async_remote_copy(
@@ -174,25 +168,21 @@
 
     loads[3].wait()
     loads[4].wait()
-
-    @pl.when(section == 0)
-    def _():
-        square = (CAP, CAP)
-        spots = lax.broadcasted_iota(jnp.int32, square, 1)
-        groups = lax.broadcasted_iota(jnp.int32, square, 0)
-        limits = jnp.sum(
-            jnp.where(spots == groups, counts[...][None].astype(F32), 0.0), axis=1, keepdims=True
-        )
-        wanted = jnp.where(spots.astype(F32) < limits, dest[...].astype(F32), -1.0)
-        flat = (CAP, SECTIONS * CAP)
-        column = lax.broadcasted_iota(jnp.int32, flat, 1)
-        line = lax.broadcasted_iota(jnp.int32, flat, 0)
-        spread_out = jnp.dot(
-            wanted.astype(BF16), (column % CAP == line).astype(BF16), preferred_element_type=F32
-        )
-        places = jnp.sum(jnp.where(column // CAP == line, spread_out, 0.0), axis=0, keepdims=True)
-        rows = lax.broadcasted_iota(jnp.int32, (ROWS, SECTIONS * CAP), 0).astype(F32)
-        onehot[...] = (rows == places).astype(BF16)
+    loads[8].wait()
+    square = (CAP, CAP)
+    lane = lax.broadcasted_iota(jnp.int32, square, 1)
+    line = lax.broadcasted_iota(jnp.int32, square, 0)
+    places = dest[...].astype(F32)
+    limit = jnp.sum(
+        jnp.where(lane[:1] == section, counts[...][None].astype(F32), 0.0), axis=1, keepdims=True
+    )
+    live = lax.broadcasted_iota(jnp.int32, (CAP, 1), 0).astype(F32) < limit
+    own_place = jnp.sum(jnp.where(line == section, places, 0.0), axis=0, keepdims=True)
+    own_place = jnp.sum(jnp.where(line == lane, own_place, 0.0), axis=1, keepdims=True)
+    position = lax.broadcasted_iota(jnp.int32, (CAP, ROWS), 1).astype(F32)
+    own_text = jnp.dot(
+        (position == own_place).astype(BF16), text_v[...], preferred_element_type=F32
+    )
 
     loads[5].wait()
     loads[6].wait()
@@ -237,42 +227,55 @@
     loads[7].wait()
     embed = jnp.dot(pooled[...], project_v[...], preferred_element_type=F32).astype(BF16)
 
+    start[...] = (
+        (own_text + jnp.where(live, embed.astype(F32), 0.0)).astype(BF16).reshape(2, R, WIDTH)
+    )
+    own_pair = pl.ds(2 * section, 2)
+
+    def class_of(slot):
+        (c,) = [c for c, (lo, hi) in enumerate(CLASSES) if lo <= slot < hi]
+        return c
+
+    def send_start(count, which):
+        for n, (i, offset) in enumerate(FAR_FIRST[:count]):
+            slot = slot_at_target(offset)
+            send(
+                start,
+                features.at[own_pair, slot],
+                feature_sem.at[2 * section, class_of(slot)],
+                targets[i],
+                start_send.at[which(n)],
+                0,
+            )
+
+    def pass_token():
+        pl.semaphore_signal(token, inc=1, device_id=(section + 1, me), device_id_type=MESH)
+
+    @pl.when(section == 0)
+    def _():
+        features[pl.ds(0, 2), 0] = start[...]
+        send_start(TP - 1, lambda n: 0)
+        pass_token()
+
     @pl.when(section > 0)
     def _():
-        embed_own[...] = embed
-        send(embed_own, embeds.at[section], phase_recv.at[4], me, phase_send.at[4], 0)
-
-    loads[8].wait()
-
-    def spread_rows(p):
-        two = pl.ds(2 * p, 2)
-        features[two, 0] = start[two]
-        for i, to in peers:
-            slot = slot_at_target(OFFSETS[i])
-            (c,) = [c for c, (lo, hi) in enumerate(CLASSES) if lo <= slot < hi]
-            send(
-                start.at[two],
-                features.at[two, slot],
-                feature_sem.at[2 * p, c],
-                to,
-                start_send.at[2 * p * BATCHES // STEPS],
-            )
-
-    @pl.when(section == 0)
-    def _():
-        embeds[0] = embed
-        arrived(embeds.at[pl.ds(0, SECTIONS - 1)], phase_recv.at[4])
-        for p in range(PAIRS):
-            rows = slice(2 * R * p, 2 * R * (p + 1))
-            placed = jnp.dot(
-                onehot[rows, :],
-                embeds[...].reshape(SECTIONS * CAP, WIDTH),
-                preferred_element_type=F32,
-            )
-            first = text_v[rows, :].astype(F32) + placed
-            start[2 * p : 2 * p + 2] = first.reshape(2, R, WIDTH).astype(BF16)
-            if p < AHEAD:
-                spread_rows(p)
+        pl.semaphore_wait(token, 1)
+        send_start(TP, lambda n: n // HALF)
+        arrived(features.at[pl.ds(0, 2), pl.ds(0, HALF)], start_send.at[0])
+
+        @pl.when(section < SECTIONS - 1)
+        def _():
+            pass_token()
+
+    flat = (CAP, ROWS)
+    column = lax.broadcasted_iota(jnp.int32, flat, 1)
+    line = lax.broadcasted_iota(jnp.int32, flat, 0)
+    spread_out = jnp.dot(
+        places.astype(BF16), (column % CAP == line).astype(BF16), preferred_element_type=F32
+    )
+    places = jnp.sum(jnp.where(column // CAP == line, spread_out, 0.0), axis=0, keepdims=True)
+    position = lax.broadcasted_iota(jnp.int32, (ROWS, ROWS), 0).astype(F32)
+    onehot[...] = (position == places).astype(BF16)
 
     arrived(gains.at[pl.ds(0, TP - 1)], phase_recv.at[1])
     arrived(weight_v, weight_sem)
@@ -294,36 +297,31 @@
     def hand_on(m):
         for i, offset in FAR_FIRST:
             slot = slot_at_target(offset)
-            (c,) = [c for c, (lo, hi) in enumerate(CLASSES) if lo <= slot < hi]
             send(
                 result.at[m],
                 features.at[m, slot],
-                feature_sem.at[m, c],
+                feature_sem.at[m, class_of(slot)],
                 targets[i],
                 layer_send.at[m * BATCHES // STEPS],
                 section + 1,
             )
 
-    def store(p):
-        two = pl.ds(2 * p, 2)
-        pltpu.make_async_copy(result.at[two], out.at[two], out_sem).start()
-
     @pl.when(section == 0)
     def _():
         def pair(p, carry):
-            @pl.when(p + AHEAD < PAIRS)
-            def _():
-                spread_rows(p + AHEAD)
-
             def wait(c, slots):
+                def both():
+                    arrived(features.at[pl.ds(2 * p, 2), slots], feature_sem.at[2 * p, c])
+
                 if c:
-                    arrived(features.at[pl.ds(2 * p, 2), slots], feature_sem.at[2 * p, c])
+                    both()
+                else:
+                    pl.when(p > 0)(both)
 
             layer(2 * p, wait)
             hand_on(2 * p)
             layer(2 * p + 1, lambda c, slots: None)
             hand_on(2 * p + 1)
-            store(p)
             return carry
 
         lax.fori_loop(0, PAIRS, pair, 0)
@@ -338,10 +336,18 @@
                 def _():
                     hand_on(m)
 
-            store(p)
             return carry
 
         lax.fori_loop(0, PAIRS, pair, 0)
+
+    pieces = []
+    for b in range(BATCHES):
+        rows = slice(b * ROWS // BATCHES, (b + 1) * ROWS // BATCHES)
+        ordered[rows, :] = jnp.dot(
+            onehot[rows, :], result[...].reshape(ROWS, WIDTH), preferred_element_type=F32
+        ).astype(BF16)
+        pieces.append(pltpu.make_async_copy(ordered.at[rows, :], out.at[rows, :], out_sem.at[b]))
+        pieces[b].start()
 
     arrived(normed.at[pl.ds(0, TP - 1)], phase_send.at[0])
     arrived(gains.at[pl.ds(0, TP - 1)], phase_send.at[1])
@@ -355,23 +361,23 @@
     def _():
         arrived(partial, phase_send.at[2])
 
+    many = STEPS // BATCHES
+
+    @pl.when(section == 0)
+    def _():
+        arrived(features.at[pl.ds(0, 2), pl.ds(0, TP - 1)], start_send.at[0])
+
     @pl.when(section > 0)
     def _():
-        arrived(embed_own, phase_send.at[4])
-
-    many = STEPS // BATCHES
-
-    @pl.when(section == 0)
-    def _():
-        for b in range(BATCHES):
-            arrived(features.at[pl.ds(b * many, many), pl.ds(0, TP - 1)], start_send.at[b])
+        arrived(features.at[pl.ds(0, 2), pl.ds(0, HALF)], start_send.at[1])
 
     @pl.when(section < SECTIONS - 1)
     def _():
         for b in range(BATCHES):
             arrived(features.at[pl.ds(b * many, many)], layer_send.at[b])
 
-    arrived(result, out_sem)
+    for piece in pieces:
+        piece.wait()
 
 
 def shards(
@@ -391,7 +397,7 @@
     hidden = vit_up.shape[1]
     outputs = pl.pallas_call(
         kernel,
-        out_shape=jax.ShapeDtypeStruct((STEPS, R, WIDTH), BF16),
+        out_shape=jax.ShapeDtypeStruct((ROWS, WIDTH), BF16),
         in_specs=[hbm] * 10,
         out_specs=hbm,
         scratch_shapes=[
@@ -409,22 +415,22 @@
             pltpu.VMEM((COLS, TP, LANES), BF16),
             pltpu.VMEM((TP, TP, LANES), BF16),
             pltpu.VMEM((TP, DV), BF16),
-            pltpu.VMEM((CAP, WIDTH), BF16),
-            pltpu.VMEM((SECTIONS, CAP, WIDTH), BF16),
-            pltpu.VMEM((ROWS, SECTIONS * CAP), BF16),
-            pltpu.VMEM((STEPS, R, WIDTH), BF16),
+            pltpu.VMEM((2, R, WIDTH), BF16),
+            pltpu.VMEM((ROWS, ROWS), BF16),
             pltpu.VMEM((1, WIDTH), F32),
             pltpu.VMEM((TP, 1, WIDTH), F32),
             pltpu.VMEM((STEPS, TP, R, WIDTH), BF16),
             pltpu.VMEM((STEPS, R, WIDTH), BF16),
+            pltpu.VMEM((ROWS, WIDTH), BF16),
             dma((9,)),
             dma,
-            dma((5,)),
-            dma((5,)),
-            dma((BATCHES,)),
+            dma((4,)),
+            dma((4,)),
+            dma((2,)),
             dma((BATCHES,)),
             dma((STEPS, len(CLASSES))),
-            dma,
+            dma((BATCHES,)),
+            pltpu.SemaphoreType.REGULAR,
         ],
         compiler_params=pltpu.CompilerParams(
             collective_id=0, has_side_effects=True, vmem_limit_bytes=60 << 20

time: 170 us -> 165 us (0.971)
  Pallas kernels: 168 us -> 163 us
    pallas_call x1, Pallas kernels: 168 us -> 163 us  [shards(): pl.pallas_call(kernel, out_shape=jax.ShapeDtypeStruct((ROWS, WIDTH), BF16...]
where the time goes in v4:
time: 165 us
  Pallas kernels  163 us (99%)
  local copies, waits for them, and re-layouts  1.67 us (1%)
    pallas_call x1, Pallas kernels, shards(): pl.pallas_call(kernel, out_shape=jax.ShapeDtypeStruct((ROWS, WIDTH), BF16...  163 us

profile of v4, /device:TPU:225, one launch (start us, length us, event | category | flops | bytes accessed | tf_op | source)
XLA Modules:
  0.0 165.0 jit_solution(9629435266404975411)
XLA Ops:
  0.0 163.3 %encoder_and_layers.1 = bf16[256,512]{1,0:T(8,128)(2,1)} custom-call(bf16[4,1664]{1,0:T(4,128)(2,1)} %patches_in.1, f32[1664]{0:T(1024)} %vit_gain_in.1, s32[16]{0:T(128)} %counts_in.1, s32[16,16]{1,0:T(8,128)} %dest_in.1, bf16[1,512]{1,0:T(2,128)(2,1)} %layer_gain_in.1, bf16[1664,256]{1,0:T(8,128)(2,1)} %vit_up.1, bf16[256,1664]{1,0:T(8,128)(2,1)} %vit_down.1, ...), custom_call_target="tpu_custom_call" | custom-call | flops 2147483648 | bytes 12582912 | tf_op jit(solution)/shard_map/encoder_and_layers/pallas_call | solution.py:398
  163.3 1.7 %copy.12 = bf16[1,8,32,512]{3,2,1,0:T(8,128)(2,1)} copy(bf16[1,8,32,512]{3,2,1,0:T(8,128)(2,1)} %bitcast.3) | data formatting | bytes 524288

commit v5 on v4

--- a/solution.py
+++ b/solution.py
@@ -73,12 +73,10 @@
     parts,
     pooled,
     start,
-    onehot,
     gain_own,
     gains,
     features,
     result,
-    ordered,
     load_sem,
     weight_sem,
     phase_send,
@@ -267,16 +265,6 @@
         def _():
             pass_token()
 
-    flat = (CAP, ROWS)
-    column = lax.broadcasted_iota(jnp.int32, flat, 1)
-    line = lax.broadcasted_iota(jnp.int32, flat, 0)
-    spread_out = jnp.dot(
-        places.astype(BF16), (column % CAP == line).astype(BF16), preferred_element_type=F32
-    )
-    places = jnp.sum(jnp.where(column // CAP == line, spread_out, 0.0), axis=0, keepdims=True)
-    position = lax.broadcasted_iota(jnp.int32, (ROWS, ROWS), 0).astype(F32)
-    onehot[...] = (position == places).astype(BF16)
-
     arrived(gains.at[pl.ds(0, TP - 1)], phase_recv.at[1])
     arrived(weight_v, weight_sem)
 
@@ -306,6 +294,10 @@
                 section + 1,
             )
 
+    def store(p):
+        two = pl.ds(2 * p, 2)
+        pltpu.make_async_copy(result.at[two], out.at[two], out_sem.at[0]).start()
+
     @pl.when(section == 0)
     def _():
         def pair(p, carry):
@@ -322,6 +314,7 @@
             hand_on(2 * p)
             layer(2 * p + 1, lambda c, slots: None)
             hand_on(2 * p + 1)
+            store(p)
             return carry
 
         lax.fori_loop(0, PAIRS, pair, 0)
@@ -336,18 +329,10 @@
                 def _():
                     hand_on(m)
 
+            store(p)
             return carry
 
         lax.fori_loop(0, PAIRS, pair, 0)
-
-    pieces = []
-    for b in range(BATCHES):
-        rows = slice(b * ROWS // BATCHES, (b + 1) * ROWS // BATCHES)
-        ordered[rows, :] = jnp.dot(
-            onehot[rows, :], result[...].reshape(ROWS, WIDTH), preferred_element_type=F32
-        ).astype(BF16)
-        pieces.append(pltpu.make_async_copy(ordered.at[rows, :], out.at[rows, :], out_sem.at[b]))
-        pieces[b].start()
 
     arrived(normed.at[pl.ds(0, TP - 1)], phase_send.at[0])
     arrived(gains.at[pl.ds(0, TP - 1)], phase_send.at[1])
@@ -376,8 +361,7 @@
         for b in range(BATCHES):
             arrived(features.at[pl.ds(b * many, many)], layer_send.at[b])
 
-    for piece in pieces:
-        piece.wait()
+    arrived(result, out_sem.at[0])
 
 
 def shards(
@@ -397,7 +381,7 @@
     hidden = vit_up.shape[1]
     outputs = pl.pallas_call(
         kernel,
-        out_shape=jax.ShapeDtypeStruct((ROWS, WIDTH), BF16),
+        out_shape=jax.ShapeDtypeStruct((STEPS, R, WIDTH), BF16),
         in_specs=[hbm] * 10,
         out_specs=hbm,
         scratch_shapes=[
@@ -416,12 +400,10 @@
             pltpu.VMEM((TP, TP, LANES), BF16),
             pltpu.VMEM((TP, DV), BF16),
             pltpu.VMEM((2, R, WIDTH), BF16),
-            pltpu.VMEM((ROWS, ROWS), BF16),
             pltpu.VMEM((1, WIDTH), F32),
             pltpu.VMEM((TP, 1, WIDTH), F32),
             pltpu.VMEM((STEPS, TP, R, WIDTH), BF16),
             pltpu.VMEM((STEPS, R, WIDTH), BF16),
-            pltpu.VMEM((ROWS, WIDTH), BF16),
             dma((9,)),
             dma,
             dma((4,)),
@@ -451,7 +433,12 @@
         text,
         layer_weight[0],
     )
-    return outputs.reshape(1, 8, ROWS // 8, WIDTH)
+    slots = outputs.reshape(SECTIONS, CAP, WIDTH)
+    onehot = (image_dest[:, :, None] == jnp.arange(ROWS, dtype=jnp.int32)).astype(BF16)
+    ordered = lax.dot_general(
+        onehot, slots, (((0, 1), (0, 1)), ((), ())), preferred_element_type=F32
+    )
+    return ordered.astype(BF16).reshape(1, 8, ROWS // 8, WIDTH)
 
 
 def solution(mesh):

time: 165 us -> 165 us (level)
  matrix products: 0 us -> 2 us
  local copies, waits for them, and re-layouts: 1.67 us -> 0.01 us
    dot_general x0 -> x1, matrix products: none -> 2 us  [shards(): lax.dot_general(onehot, slots, (((0, 1), (0, 1)), ((), ())), preferred_el...]
    unnamed x1 -> x2, local copies, waits for them, and re-layouts: 1.67 us -> 0.01 us
where the time goes in v5:
time: 165 us
  Pallas kernels  163 us (99%)
  matrix products  2 us (1%)
    pallas_call x1, Pallas kernels, shards(): pl.pallas_call(kernel, out_shape=jax.ShapeDtypeStruct((STEPS, R, WIDTH),...  163 us

profile of v5, /device:TPU:225, one launch (start us, length us, event | category | flops | bytes accessed | tf_op | source)
XLA Modules:
  0.0 164.5 jit_solution(9800379453852691278)
XLA Ops:
  0.0 0.0 copy-start
  0.0 162.5 %encoder_and_layers.1 = bf16[32,8,512]{2,1,0:T(8,128)(2,1)} custom-call(bf16[4,1664]{1,0:T(4,128)(2,1)} %patches_in.1, f32[1664]{0:T(1024)} %vit_gain_in.1, s32[16]{0:T(128)} %counts_in.1, s32[16,16]{1,0:T(8,128)} %dest_in.1, bf16[1,512]{1,0:T(2,128)(2,1)} %layer_gain_in.1, bf16[1664,256]{1,0:T(8,128)(2,1)} %vit_up.1, bf16[256,1664]{1,0:T(8,128)(2,1)} %vit_down.1, ...), custom_call_target="tpu_custom_call" | custom-call | flops 2147483648 | bytes 12582912 | tf_op jit(solution)/shard_map/encoder_and_layers/pallas_call | solution.py:382
  162.5 0.0 copy-done
  162.5 2.0 %fusion = bf16[256,512]{1,0:T(8,128)(2,1)} fusion(bf16[16,16,512]{2,1,0:T(8,128)(2,1)} %bitcast.9, s32[16,16]{1,0:T(8,128)S(1)} %copy-done), kind=kOutput, calls=%fused_computation.1 | convolution fusion | flops 67305472 | bytes 525312 | tf_op jit(solution)/shard_map/dot_general | solution.py:438
Async XLA Ops:
  0.0 162.5 %copy-start = (s32[16,16]{1,0:T(8,128)S(1)}, s32[16,16]{1,0:T(8,128)}, u32[]{:S(2)}) copy-start(s32[16,16]{1,0:T(8,128)} %dest_in.1) | copy-start | bytes 3076

commit v6 on v5

--- a/solution.py
+++ b/solution.py
@@ -26,7 +26,6 @@
 R = 8
 STEPS = ROWS // R
 PAIRS = STEPS // 2
-HALF = TP // 2
 BATCHES = 4
 
 
@@ -228,23 +227,23 @@
     start[...] = (
         (own_text + jnp.where(live, embed.astype(F32), 0.0)).astype(BF16).reshape(2, R, WIDTH)
     )
-    own_pair = pl.ds(2 * section, 2)
 
     def class_of(slot):
         (c,) = [c for c, (lo, hi) in enumerate(CLASSES) if lo <= slot < hi]
         return c
 
-    def send_start(count, which):
-        for n, (i, offset) in enumerate(FAR_FIRST[:count]):
-            slot = slot_at_target(offset)
-            send(
-                start,
-                features.at[own_pair, slot],
-                feature_sem.at[2 * section, class_of(slot)],
-                targets[i],
-                start_send.at[which(n)],
-                0,
-            )
+    def send_start(count):
+        for k in range(2):
+            for i, offset in FAR_FIRST[:count]:
+                slot = slot_at_target(offset)
+                send(
+                    start.at[k],
+                    features.at[2 * section + k, slot],
+                    feature_sem.at[2 * section + k, class_of(slot)],
+                    targets[i],
+                    start_send.at[k],
+                    0,
+                )
 
     def pass_token():
         pl.semaphore_signal(token, inc=1, device_id=(section + 1, me), device_id_type=MESH)
@@ -252,14 +251,14 @@
     @pl.when(section == 0)
     def _():
         features[pl.ds(0, 2), 0] = start[...]
-        send_start(TP - 1, lambda n: 0)
+        send_start(TP - 1)
         pass_token()
 
     @pl.when(section > 0)
     def _():
         pl.semaphore_wait(token, 1)
-        send_start(TP, lambda n: n // HALF)
-        arrived(features.at[pl.ds(0, 2), pl.ds(0, HALF)], start_send.at[0])
+        send_start(TP)
+        arrived(features.at[0], start_send.at[0])
 
         @pl.when(section < SECTIONS - 1)
         def _():
@@ -298,41 +297,28 @@
         two = pl.ds(2 * p, 2)
         pltpu.make_async_copy(result.at[two], out.at[two], out_sem.at[0]).start()
 
-    @pl.when(section == 0)
-    def _():
-        def pair(p, carry):
+    def pair(p, carry):
+        for m in (2 * p, 2 * p + 1):
+
             def wait(c, slots):
-                def both():
-                    arrived(features.at[pl.ds(2 * p, 2), slots], feature_sem.at[2 * p, c])
+                def one():
+                    arrived(features.at[m, slots], feature_sem.at[m, c])
 
                 if c:
-                    both()
+                    one()
                 else:
-                    pl.when(p > 0)(both)
-
-            layer(2 * p, wait)
-            hand_on(2 * p)
-            layer(2 * p + 1, lambda c, slots: None)
-            hand_on(2 * p + 1)
-            store(p)
-            return carry
-
-        lax.fori_loop(0, PAIRS, pair, 0)
-
-    @pl.when(section > 0)
-    def _():
-        def pair(p, carry):
-            for m in (2 * p, 2 * p + 1):
-                layer(m, lambda c, slots: arrived(features.at[m, slots], feature_sem.at[m, c]))
-
-                @pl.when(section < SECTIONS - 1)
-                def _():
-                    hand_on(m)
-
-            store(p)
-            return carry
-
-        lax.fori_loop(0, PAIRS, pair, 0)
+                    pl.when((section > 0) | (p > 0))(one)
+
+            layer(m, wait)
+
+            @pl.when(section < SECTIONS - 1)
+            def _():
+                hand_on(m)
+
+        store(p)
+        return carry
+
+    lax.fori_loop(0, PAIRS, pair, 0)
 
     arrived(normed.at[pl.ds(0, TP - 1)], phase_send.at[0])
     arrived(gains.at[pl.ds(0, TP - 1)], phase_send.at[1])
@@ -350,11 +336,12 @@
 
     @pl.when(section == 0)
     def _():
-        arrived(features.at[pl.ds(0, 2), pl.ds(0, TP - 1)], start_send.at[0])
+        for k in range(2):
+            arrived(features.at[k, pl.ds(0, TP - 1)], start_send.at[k])
 
     @pl.when(section > 0)
     def _():
-        arrived(features.at[pl.ds(0, 2), pl.ds(0, HALF)], start_send.at[1])
+        arrived(features.at[1], start_send.at[1])
 
     @pl.when(section < SECTIONS - 1)
     def _():

time: 165 us -> 162 us (0.982)
  Pallas kernels: 163 us -> 160 us
    pallas_call x1, Pallas kernels: 163 us -> 160 us  [shards(): pl.pallas_call(kernel, out_shape=jax.ShapeDtypeStruct((STEPS, R, WIDTH),...]
where the time goes in v6:
time: 162 us
  Pallas kernels  160 us (99%)
  matrix products  2 us (1%)
    pallas_call x1, Pallas kernels, shards(): pl.pallas_call(kernel, out_shape=jax.ShapeDtypeStruct((STEPS, R, WIDTH),...  160 us

profile of v6, /device:TPU:225, one launch (start us, length us, event | category | flops | bytes accessed | tf_op | source)
XLA Modules:
  0.0 161.8 jit_solution(13115810593196605787)
XLA Ops:
  0.0 0.0 copy-start
  0.0 159.8 %encoder_and_layers.1 = bf16[32,8,512]{2,1,0:T(8,128)(2,1)} custom-call(bf16[4,1664]{1,0:T(4,128)(2,1)} %patches_in.1, f32[1664]{0:T(1024)} %vit_gain_in.1, s32[16]{0:T(128)} %counts_in.1, s32[16,16]{1,0:T(8,128)} %dest_in.1, bf16[1,512]{1,0:T(2,128)(2,1)} %layer_gain_in.1, bf16[1664,256]{1,0:T(8,128)(2,1)} %vit_up.1, bf16[256,1664]{1,0:T(8,128)(2,1)} %vit_down.1, ...), custom_call_target="tpu_custom_call" | custom-call | flops 2147483648 | bytes 12582912 | tf_op jit(solution)/shard_map/encoder_and_layers/pallas_call | solution.py:369
  159.8 0.0 copy-done
  159.8 2.0 %fusion = bf16[256,512]{1,0:T(8,128)(2,1)} fusion(bf16[16,16,512]{2,1,0:T(8,128)(2,1)} %bitcast.9, s32[16,16]{1,0:T(8,128)S(1)} %copy-done), kind=kOutput, calls=%fused_computation.1 | convolution fusion | flops 67305472 | bytes 525312 | tf_op jit(solution)/shard_map/dot_general | solution.py:425
Async XLA Ops:
  0.0 159.8 %copy-start = (s32[16,16]{1,0:T(8,128)S(1)}, s32[16,16]{1,0:T(8,128)}, u32[]{:S(2)}) copy-start(s32[16,16]{1,0:T(8,128)} %dest_in.1) | copy-start | bytes 3076

commit v7 on v6

--- a/solution.py
+++ b/solution.py
@@ -26,6 +26,7 @@
 R = 8
 STEPS = ROWS // R
 PAIRS = STEPS // 2
+EARLY = 12
 BATCHES = 4
 
 
@@ -39,6 +40,8 @@
     (lo, lo + sum(hops(o) == h for o in OFFSETS))
     for h, lo in [(hops(o), i) for i, o in enumerate(OFFSETS) if i == 0 or hops(o) != hops(OFFSETS[i - 1])]
 ]
+
+ORDER = (0, 1, 3, 4, 2)
 
 
 def slot_at_target(offset):
@@ -234,14 +237,14 @@
 
     def send_start(count):
         for k in range(2):
-            for i, offset in FAR_FIRST[:count]:
+            for n, (i, offset) in enumerate(FAR_FIRST[:count]):
                 slot = slot_at_target(offset)
                 send(
                     start.at[k],
                     features.at[2 * section + k, slot],
                     feature_sem.at[2 * section + k, class_of(slot)],
                     targets[i],
-                    start_send.at[k],
+                    start_send.at[0 if k == 0 and n < EARLY else 1],
                     0,
                 )
 
@@ -258,7 +261,7 @@
     def _():
         pl.semaphore_wait(token, 1)
         send_start(TP)
-        arrived(features.at[0], start_send.at[0])
+        arrived(features.at[0, pl.ds(0, EARLY)], start_send.at[0])
 
         @pl.when(section < SECTIONS - 1)
         def _():
@@ -270,7 +273,8 @@
     def layer(m, wait):
         product = jnp.zeros((R, WIDTH), F32)
         squares = jnp.zeros((R, LANES), F32)
-        for c, (lo, hi) in enumerate(CLASSES):
+        for c in ORDER:
+            lo, hi = CLASSES[c]
             wait(c, pl.ds(lo, hi - lo))
             for i in range(lo, hi):
                 part = features[m, i].astype(F32)
@@ -336,11 +340,13 @@
 
     @pl.when(section == 0)
     def _():
-        for k in range(2):
-            arrived(features.at[k, pl.ds(0, TP - 1)], start_send.at[k])
+        arrived(features.at[0, pl.ds(0, EARLY)], start_send.at[0])
+        arrived(features.at[0, pl.ds(EARLY, TP - 1 - EARLY)], start_send.at[1])
+        arrived(features.at[1, pl.ds(0, TP - 1)], start_send.at[1])
 
     @pl.when(section > 0)
     def _():
+        arrived(features.at[0, pl.ds(EARLY, TP - EARLY)], start_send.at[1])
         arrived(features.at[1], start_send.at[1])
 
     @pl.when(section < SECTIONS - 1)

time: 162 us -> 161 us (level)
  no operation moved by 1% of the time
where the time goes in v7:
time: 161 us
  Pallas kernels  159 us (99%)
  matrix products  2 us (1%)
    pallas_call x1, Pallas kernels, shards(): pl.pallas_call(kernel, out_shape=jax.ShapeDtypeStruct((STEPS, R, WIDTH),...  159 us

profile of v7, /device:TPU:225, one launch (start us, length us, event | category | flops | bytes accessed | tf_op | source)
XLA Modules:
  0.0 160.7 jit_solution(10726426981340605242)
XLA Ops:
  0.0 0.0 copy-start
  0.0 158.7 %encoder_and_layers.1 = bf16[32,8,512]{2,1,0:T(8,128)(2,1)} custom-call(bf16[4,1664]{1,0:T(4,128)(2,1)} %patches_in.1, f32[1664]{0:T(1024)} %vit_gain_in.1, s32[16]{0:T(128)} %counts_in.1, s32[16,16]{1,0:T(8,128)} %dest_in.1, bf16[1,512]{1,0:T(2,128)(2,1)} %layer_gain_in.1, bf16[1664,256]{1,0:T(8,128)(2,1)} %vit_up.1, bf16[256,1664]{1,0:T(8,128)(2,1)} %vit_down.1, ...), custom_call_target="tpu_custom_call" | custom-call | flops 2147483648 | bytes 12582912 | tf_op jit(solution)/shard_map/encoder_and_layers/pallas_call | solution.py:375
  158.7 0.0 copy-done
  158.7 2.0 %fusion = bf16[256,512]{1,0:T(8,128)(2,1)} fusion(bf16[16,16,512]{2,1,0:T(8,128)(2,1)} %bitcast.9, s32[16,16]{1,0:T(8,128)S(1)} %copy-done), kind=kOutput, calls=%fused_computation.1 | convolution fusion | flops 67305472 | bytes 525312 | tf_op jit(solution)/shard_map/dot_general | solution.py:431
Async XLA Ops:
  0.0 158.7 %copy-start = (s32[16,16]{1,0:T(8,128)S(1)}, s32[16,16]{1,0:T(8,128)}, u32[]{:S(2)}) copy-start(s32[16,16]{1,0:T(8,128)} %dest_in.1) | copy-start | bytes 3076

commit v8 on v7

--- a/solution.py
+++ b/solution.py
@@ -102,13 +102,13 @@
     def greet(to_section, to):
         pl.semaphore_signal(barrier, inc=1, device_id=(to_section, to), device_id_type=MESH)
 
+    @pl.when(section > 0)
+    def _():
+        for i, _ in FAR_FIRST:
+            greet(section - 1, targets[i])
+
     for _, to in peers:
         greet(section, to)
-
-    @pl.when(section > 0)
-    def _():
-        for i, _ in FAR_FIRST:
-            greet(section - 1, targets[i])
 
     loads = [
         pltpu.make_async_copy(source, target, load_sem.at[i])

time: 161 us -> 161 us (level)
  no operation moved by 1% of the time
where the time goes in v8:
time: 161 us
  Pallas kernels  159 us (99%)
  matrix products  2 us (1%)
    pallas_call x1, Pallas kernels, shards(): pl.pallas_call(kernel, out_shape=jax.ShapeDtypeStruct((STEPS, R, WIDTH),...  159 us

profile of v8, /device:TPU:225, one launch (start us, length us, event | category | flops | bytes accessed | tf_op | source)
XLA Modules:
  0.0 160.7 jit_solution(11222569035863102935)
XLA Ops:
  0.0 0.0 copy-start
  0.0 158.7 %encoder_and_layers.1 = bf16[32,8,512]{2,1,0:T(8,128)(2,1)} custom-call(bf16[4,1664]{1,0:T(4,128)(2,1)} %patches_in.1, f32[1664]{0:T(1024)} %vit_gain_in.1, s32[16]{0:T(128)} %counts_in.1, s32[16,16]{1,0:T(8,128)} %dest_in.1, bf16[1,512]{1,0:T(2,128)(2,1)} %layer_gain_in.1, bf16[1664,256]{1,0:T(8,128)(2,1)} %vit_up.1, bf16[256,1664]{1,0:T(8,128)(2,1)} %vit_down.1, ...), custom_call_target="tpu_custom_call" | custom-call | flops 2147483648 | bytes 12582912 | tf_op jit(solution)/shard_map/encoder_and_layers/pallas_call | solution.py:375
  158.7 0.0 copy-done
  158.7 2.0 %fusion = bf16[256,512]{1,0:T(8,128)(2,1)} fusion(bf16[16,16,512]{2,1,0:T(8,128)(2,1)} %bitcast.9, s32[16,16]{1,0:T(8,128)S(1)} %copy-done), kind=kOutput, calls=%fused_computation.1 | convolution fusion | flops 67305472 | bytes 525312 | tf_op jit(solution)/shard_map/dot_general | solution.py:431
Async XLA Ops:
  0.0 158.7 %copy-start = (s32[16,16]{1,0:T(8,128)S(1)}, s32[16,16]{1,0:T(8,128)}, u32[]{:S(2)}) copy-start(s32[16,16]{1,0:T(8,128)} %dest_in.1) | copy-start | bytes 3076
